TPU v7x, 512 devices: a whole 4x4x16 slice. The times are simulated.
512 devices in a mesh: query: 4 (over x), ctx: 32 (over z_lo, y), ffn: 4 (over z_hi, core).
Axes of the slice: x: 4, y: 4, z: 16 (z_hi: 2, z_lo: 8; z = z_hi * 8 + z_lo), core: 2. Of those that a mesh axis runs over, the one named last changes fastest.
Arguments:
- token_grads: bfloat16 [12288, 14336], P('ctx', 'ffn'), may hold values from -6 to 6
- token_inputs: bfloat16 [12288, 4096], P('ctx', 'ffn'), may hold values from -6 to 6
- up_factors: bfloat16 [4096, 14336], P(('query', 'ctx'), 'ffn'), may hold values from -0.0078125 to 0.0078125
- in_factors: bfloat16 [4096, 4096], P(('query', 'ctx'), 'ffn'), may hold values from -0.09375 to 0.09375
- loss_mask: int32 [12288], P('ctx'), may hold values 0 or 1
Outputs:
- scores: float32 [12288, 128], P(('ctx', 'ffn'), 'query')
All inputs are finite; a program needn't handle non-finite values. No bound on the sum of `loss_mask` on one device may be relied on, other than what follows from the above.
Results may differ from a plain program's by a relative error of at most 0.0003.
Values may be sent and summed in bfloat16 or wider, within the bound.
No kernel may reach another device: no remote copies, remote signals or barrier semaphores. Data moves between devices by JAX's collectives and lax.ppermute only.
A program may use at most 64 MiB of HBM per device.

v0:
```python
import jax
import jax.numpy as jnp
from jax import lax
from jax.sharding import PartitionSpec as P

RANK = 32


def contract(data_rows, factor_rows):
    return lax.dot_general(
        data_rows, factor_rows, (((1,), (1,)), ((), ())), preferred_element_type=jnp.float32
    )


def body(token_grads, token_inputs, up_factors, in_factors, loss_mask):
    up_gathered, in_gathered = (
        lax.all_gather(up_factors, "ctx", axis=0, tiled=True),
        lax.all_gather(in_factors, "ctx", axis=0, tiled=True),
    )
    row_count = token_grads.shape[0]
    share_rows = row_count // lax.axis_size("ffn")
    offset = lax.axis_index("ffn") * share_rows
    factor_rows = up_gathered.shape[0]
    left_full = contract(token_grads, up_gathered)
    right_full = contract(token_inputs, in_gathered)
    left_full, right_full = lax.psum((left_full, right_full), "ffn")
    left_proj = lax.dynamic_slice_in_dim(left_full, offset, share_rows, 0)
    right_proj = lax.dynamic_slice_in_dim(right_full, offset, share_rows, 0)
    own_mask = lax.dynamic_slice_in_dim(loss_mask, offset, share_rows, 0)
    summed = (left_proj * right_proj).reshape(share_rows, factor_rows // RANK, RANK).sum(axis=2)
    return summed * own_mask.astype(jnp.float32)[:, None]


def solution(mesh):
    in_specs = (
        P("ctx", "ffn"),
        P("ctx", "ffn"),
        P(("query", "ctx"), "ffn"),
        P(("query", "ctx"), "ffn"),
        P("ctx"),
    )
    out_specs = P(("ctx", "ffn"), "query")
    return jax.shard_map(body, mesh=mesh, in_specs=in_specs, out_specs=out_specs, check_vma=False)
```

profile of v0, /device:TPU:97, one launch (start us, length us, event | category | flops | bytes accessed | tf_op | source)
XLA Modules:
  0.0 739.7 jit_solution(2531359624776107432)
XLA Ops:
  6.5 0.0 copy-start
  6.5 0.0 all-gather.5.cloned.1.call-start
  6.5 0.7 all-gather.5.cloned.1.call-update
  7.3 0.0 all-gather.3.cloned.1.call-start
  7.3 0.7 all-gather.3.cloned.1.call-update
  8.0 0.0 all-reduce.3.cloned.1.call-start
  8.1 168.1 %all-gather.5.cloned.1.call-done = bf16[1024,1024]{1,0:T(8,128)(2,1)} async-done(((bf16[32,1024]{1,0:T(8,128)(2,1)}), bf16[1024,1024]{1,0:T(8,128)(2,1)}) %all-gather.5.cloned.1.call-update) | async-done | bytes 2097168 | tf_op jit(solution)/shard_map/all_gather | solution.py:18
  176.1 4.0 fusion.1
  180.2 232.3 %all-gather.3.cloned.1.call-done = bf16[1024,3584]{1,0:T(8,128)(2,1)} async-done(((bf16[32,3584]{1,0:T(8,128)(2,1)}), bf16[1024,3584]{1,0:T(8,128)(2,1)}) %all-gather.3.cloned.1.call-update) | async-done | bytes 7340048 | tf_op jit(solution)/shard_map/all_gather | solution.py:17
  412.5 0.0 copy-done
  412.5 7.3 fusion
  419.8 0.0 all-reduce.3.cloned.1.call-update
  419.9 0.8 dynamic-slice_convert_fusion
  420.6 308.8 %all-reduce.3.cloned.1.call-done = (f32[384,1024]{1,0:T(8,128)}, f32[384,1024]{1,0:T(8,128)}) async-done(((f32[384,1024]{1,0:T(8,128)}, f32[384,1024]{1,0:T(8,128)}), (f32[384,1024]{1,0:T(8,128)}, f32[384,1024]{1,0:T(8,128)})) %all-reduce.3.cloned.1.call-update) | async-done | bytes 3145744 | tf_op jit(solution)/shard_map/psum | solution.py:26
  729.4 1.9 dynamic-slice_multiply_fusion
  731.3 1.2 copy.6
  732.5 0.1 bitcast_reduce_fusion
  732.6 0.6 broadcast_multiply_fusion
Async XLA Ops:
  6.5 405.9 %copy-start = (bf16[384,3584]{1,0:T(8,128)(2,1)S(1)}, bf16[384,3584]{1,0:T(8,128)(2,1)}, u32[]{:S(2)}) copy-start(bf16[384,3584]{1,0:T(8,128)(2,1)} %param.5) | copy-start | bytes 8257540
  6.5 169.6 %all-gather.5.cloned.1.call-start = ((), (), s32[]{:S(2)}) async-start(), calls=%async_computation.1 | async-start | bytes 2162688 | tf_op jit(solution)/shard_map/all_gather | solution.py:18
  7.3 405.2 %all-gather.3.cloned.1.call-start = ((), (), s32[]{:S(2)}) async-start(), calls=%async_computation | async-start | bytes 7569408 | tf_op jit(solution)/shard_map/all_gather | solution.py:17
  8.0 721.4 %all-reduce.3.cloned.1.call-start = ((), (), s32[]{:S(2)}) async-start(), calls=%async_computation.2 | async-start | bytes 6291456 | tf_op jit(solution)/shard_map/psum | solution.py:26
Sparse Core Ops, SparseCore 0:
  9.4 166.6 all-gather.4
  178.2 234.2 all-gather.2
  420.0 309.3 all-reduce.2
where the time goes:
time: 740 us
  waiting for transfers between devices  711 us (96%)
  between operations  13.1 us (2%)
  matrix products  11.4 us (2%)
    psum x1, waiting for transfers between devices, body(): left_full, right_full = lax.psum((left_full, right_full), 'ffn')  309 us
    all_gather x1, waiting for transfers between devices, body(): lax.all_gather(up_factors, 'ctx', axis=0, tiled=True)  232 us
    all_gather x1, waiting for transfers between devices, body(): lax.all_gather(in_factors, 'ctx', axis=0, tiled=True)  168 us
  transfers between devices with their start and end apart: 3, of which 3 were waited for; matrix products, arithmetic and copies ran while one was open for 1% of the time, Pallas kernels for 0%

commit v1 on v0

v1 whole, which is shorter than its diff:
```python
import jax
import jax.numpy as jnp
from jax import lax
from jax.sharding import Mesh, PartitionSpec as P

RANK = 32
HALF = RANK // 2
SWAP = ((0, 1), (1, 0))
Z_STEPS = (2, 1)
Z_OFFSETS = (0, 2, 1, 3)
Y_OFFSETS = (0, -1, 1, 2)


def rows_of(data_rows, factor_rows):
    return lax.dot_general(factor_rows, data_rows, (((1,), (1,)), ((), ())), preferred_element_type=jnp.float32)


def shift(value, axis, by):
    return lax.ppermute(value, axis, [((i + by) % 4, i) for i in range(4)])


def flip(value, axis, bits):
    return lax.ppermute(value, axis, [(i, i ^ bits) for i in range(lax.axis_size(axis))])


def swap(value, axis):
    return lax.ppermute(value, axis, SWAP)


def gather_z(block):
    for bits in Z_STEPS:
        block = jnp.concatenate([block, flip(block, "z_quad", bits)], axis=0)
    return block


def gather_y(block):
    return [block] + [shift(block, "y", by) for by in Y_OFFSETS[1:]]


def pair_rows(rows, x_at):
    quarter = rows.shape[0] // 4
    part = swap(lax.dynamic_slice_in_dim(rows, x_at * quarter, quarter, 0), "z_pair")
    return jnp.concatenate([rows, part] + [shift(part, "query", by) for by in (1, 2, 3)], axis=0)


def sum_over_halves(partial):
    count, tokens = partial.shape[0] // HALF, partial.shape[1]
    blocks = partial.reshape(count, HALF, tokens)
    largest = jnp.max(jnp.abs(blocks), axis=1)
    exponent = jnp.clip(jnp.ceil(jnp.log2(jnp.maximum(largest, 1e-30)) + 0.01), -100.0, 100.0)
    coded = jnp.round(blocks * (jnp.exp2(-exponent) * 32766.0)[:, None, :]).astype(jnp.int16)
    sent = jnp.concatenate([coded.reshape(count * HALF, tokens), exponent.astype(jnp.int16)], axis=0)
    got = swap(sent, "z_half").astype(jnp.float32)
    scale = jnp.exp2(got[count * HALF :]) * (1.0 / 32766.0)
    other = got[: count * HALF].reshape(count, HALF, tokens) * scale[:, None, :]
    return blocks + other


def body(token_grads, token_inputs, up_factors, in_factors, loss_mask):
    x_at, y_at, core = lax.axis_index("query"), lax.axis_index("y"), lax.axis_index("core")
    z_half, z_pair = lax.axis_index("z_half"), lax.axis_index("z_pair")
    hidden, features = token_grads.shape[1], token_inputs.shape[1]
    tokens = token_grads.shape[0]
    quarter = tokens // 4

    both = jnp.concatenate([in_factors, up_factors], axis=1)
    kept = lax.dynamic_slice_in_dim(both, core * HALF, HALF, 0)
    got = swap(lax.dynamic_slice_in_dim(both, (1 - core) * HALF, HALF, 0), "core")
    in_block = jnp.concatenate([kept[:, :features], got[:, :features]], axis=1)
    up_block = jnp.concatenate([kept[:, features:], got[:, features:]], axis=1)

    in_all = jnp.concatenate(gather_y(gather_z(in_block)), axis=0)
    inputs = pair_rows(token_inputs, x_at)
    inputs_other = swap(inputs, "core")
    right = rows_of(inputs, in_all[:, :features]) + rows_of(inputs_other, in_all[:, features:])
    right = sum_over_halves(right)

    up_all = jnp.concatenate(gather_y(gather_z(up_block)), axis=0)
    grads = pair_rows(token_grads, x_at)
    grads_other = swap(grads, "core")
    left = rows_of(grads, up_all[:, :hidden]) + rows_of(grads_other, up_all[:, hidden:])

    count = right.shape[0]
    summed = (left.reshape(right.shape) * right).sum(axis=1)
    parts = summed.reshape(count, 2, 4, quarter).transpose(2, 1, 0, 3)
    own, other = parts[:, 0], parts[:, 1]
    other = lax.dynamic_slice_in_dim(jnp.concatenate([other, other], axis=0), (4 - x_at) % 4, 4, 0)
    parts = jnp.stack([own, other], axis=1).reshape(2, 2, 2, count, quarter)

    mine = lax.dynamic_index_in_dim(parts, core, 1, keepdims=False)
    theirs = lax.dynamic_index_in_dim(parts, 1 - core, 1, keepdims=False)
    mine = mine + swap(theirs, "core")
    mine = jnp.stack([mine[:, 0], swap(mine[:, 1], "z_pair")], axis=1)
    result = lax.dynamic_index_in_dim(mine, z_half, 0, keepdims=False)
    result = result + swap(lax.dynamic_index_in_dim(mine, 1 - z_half, 0, keepdims=False), "z_half")
    result = result.reshape(2 * count, quarter)

    at = lax.broadcasted_iota(jnp.int32, (2 * count, 2 * count), 0)
    column = lax.broadcasted_iota(jnp.int32, (2 * count, 2 * count), 1)
    quads = len(Z_OFFSETS)
    z_quad = lax.axis_index("z_quad")
    place = jnp.zeros_like(at)
    for j, y_by in enumerate(Y_OFFSETS):
        for k, bits in enumerate(Z_OFFSETS):
            for pair in range(2):
                row = pair * count + j * quads + k
                to = ((z_quad ^ bits) * 2 + (z_pair ^ pair)) * 4 + (y_at + y_by) % 4
                place = place + jnp.where(at == row, to, 0)
    select = (place == column).astype(jnp.float32)
    scores = lax.dot_general(
        result, select, (((0,), (0,)), ((), ())), precision=lax.Precision.HIGHEST, preferred_element_type=jnp.float32
    )
    share = lax.dynamic_slice_in_dim(loss_mask, (z_half * 2 + core) * quarter, quarter, 0)
    return scores * share.astype(jnp.float32)[:, None]


def solution(mesh):
    devices = mesh.devices.reshape(4, 4, 2, 4, 2, 2)
    split = Mesh(devices, ("query", "z_quad", "z_pair", "y", "z_half", "core"))
    ctx, ffn = ("z_quad", "z_pair", "y"), ("z_half", "core")
    in_specs = (
        P(ctx, ffn),
        P(ctx, ffn),
        P(("query",) + ctx, ffn),
        P(("query",) + ctx, ffn),
        P(ctx),
    )
    return jax.shard_map(body, mesh=split, in_specs=in_specs, out_specs=P(ctx + ffn, "query"), check_vma=False)
```

time: 740 us -> 254 us (0.34)
  the two profiles are of different devices: /device:TPU:97 before, /device:TPU:56 now
where the time goes in v1:
time: 254 us; the launch traced here: 253 us
  waiting for transfers between devices  147 us (58%)
  starting transfers between devices  90.1 us (35%)
  local copies, waits for them, and re-layouts  8.29 us (3%)
  matrix products  5.47 us (2%)
    ppermute x12, waiting for transfers between devices, shift(): return lax.ppermute(value, axis, [((i + by) % 4, i) for i in range(4)])  74.4 us
    ppermute x9, waiting for transfers between devices, swap(): return lax.ppermute(value, axis, SWAP)  50.1 us
    ppermute x12, starting transfers between devices, shift(): return lax.ppermute(value, axis, [((i + by) % 4, i) for i in range(4)])  39.4 us
    ppermute x9, starting transfers between devices, swap(): return lax.ppermute(value, axis, SWAP)  35 us
    ppermute x4, waiting for transfers between devices, flip(): lax.ppermute(value, axis, [(i, i ^ bits) for i in range(lax.axis_size(axi...  22.5 us
    ppermute x4, starting transfers between devices, flip(): lax.ppermute(value, axis, [(i, i ^ bits) for i in range(lax.axis_size(axi...  15.7 us
  transfers between devices with their start and end apart: 25, of which 11 were waited for; matrix products, arithmetic and copies ran while one was open for 4% of the time, Pallas kernels for 0%

profile of v1, /device:TPU:56, one launch (start us, length us, event | category | flops | bytes accessed | tf_op | source)
XLA Modules:
  0.0 253.1 jit_solution(368044125041782786)
XLA Ops:
  8.0 3.8 %collective-permute-start.16 = (bf16[96,1024]{1,0:T(8,128)(2,1)S(1)}, bf16[96,1024]{1,0:T(8,128)(2,1)S(1)}, u32[]{:S(2)}, u32[]{:S(2)}) collective-permute-start(bf16[96,1024]{1,0:T(8,128)(2,1)S(1)} %constant_dynamic-slice_fusion), channel_id=1, source_target_pairs={{0,16},{16,0},{1,17},{17,1},{2,18},{18,2},{3,19},{19,3},{4,20},{20... | collective-permute-start | bytes 589832 | tf_op jit(solution)/shard_map/ppermute | solution.py:27
  11.8 3.5 %constant_dynamic-update-slice_fusion.12 = bf16[768,3584]{1,0:T(8,128)(2,1)} fusion(bf16[384,3584]{1,0:T(8,128)(2,1)} %param.5), kind=kLoop, calls=%fused_computation.40 | loop fusion | bytes 5505024
  15.5 9.4 %collective-permute-start.1 = (bf16[16,7168]{1,0:T(8,128)(2,1)S(1)}, bf16[16,7168]{1,0:T(8,128)(2,1)S(1)}, u32[]{:S(2)}, u32[]{:S(2)}) collective-permute-start(bf16[16,7168]{1,0:T(8,128)(2,1)S(1)} %get-tuple-element.5), channel_id=1, source_target_pairs={{0,64},{32,96},{64,0},{96,32},{1,65},{33,97},{65,1},{97,33},{2,66}... | collective-permute-start | bytes 688136 | tf_op jit(solution)/shard_map/ppermute | solution.py:23
  26.8 2.7 %collective-permute-done.16 = bf16[96,1024]{1,0:T(8,128)(2,1)S(1)} collective-permute-done((bf16[96,1024]{1,0:T(8,128)(2,1)S(1)}, bf16[96,1024]{1,0:T(8,128)(2,1)S(1)}, u32[]{:S(2)}, u32[]{:S(2)}) %collective-permute-start.16) | collective-permute-done | bytes 196640 | tf_op jit(solution)/shard_map/ppermute | solution.py:27
  29.5 4.7 %collective-permute-start.17 = (bf16[96,1024]{1,0:T(8,128)(2,1)S(1)}, bf16[96,1024]{1,0:T(8,128)(2,1)S(1)}, u32[]{:S(2)}, u32[]{:S(2)}) collective-permute-start(bf16[96,1024]{1,0:T(8,128)(2,1)S(1)} %collective-permute-done.16), channel_id=1, source_target_pairs={{128,0},{256,128},{384,256},{0,384},{129,1},{257,129},{385,257},{1... | collective-permute-start | bytes 589832 | tf_op jit(solution)/shard_map/ppermute | solution.py:19
  34.2 2.7 %collective-permute-start.18 = (bf16[96,1024]{1,0:T(8,128)(2,1)S(1)}, bf16[96,1024]{1,0:T(8,128)(2,1)S(1)}, u32[]{:S(2)}, u32[]{:S(2)}) collective-permute-start(bf16[96,1024]{1,0:T(8,128)(2,1)S(1)} %collective-permute-done.16), channel_id=1, source_target_pairs={{256,0},{384,128},{0,256},{128,384},{257,1},{385,129},{1,257},{129... | collective-permute-start | bytes 589832 | tf_op jit(solution)/shard_map/ppermute | solution.py:19
  36.9 16.5 %collective-permute-done.11 = bf16[16,2048]{1,0:T(8,128)(2,1)S(1)} collective-permute-done((bf16[16,2048]{1,0:T(8,128)(2,1)S(1)}, bf16[16,2048]{1,0:T(8,128)(2,1)S(1)}, u32[]{:S(2)}, u32[]{:S(2)}) %collective-permute-start.11) | collective-permute-done | bytes 65568 | tf_op jit(solution)/shard_map/ppermute | solution.py:23
  55.3 6.1 %collective-permute-done.12 = bf16[32,2048]{1,0:T(8,128)(2,1)S(1)} collective-permute-done((bf16[32,2048]{1,0:T(8,128)(2,1)S(1)}, bf16[32,2048]{1,0:T(8,128)(2,1)S(1)}, u32[]{:S(2)}, u32[]{:S(2)}) %collective-permute-start.12) | collective-permute-done | bytes 131104 | tf_op jit(solution)/shard_map/ppermute | solution.py:23
  61.4 3.4 %collective-permute-start.19 = (bf16[96,1024]{1,0:T(8,128)(2,1)S(1)}, bf16[96,1024]{1,0:T(8,128)(2,1)S(1)}, u32[]{:S(2)}, u32[]{:S(2)}) collective-permute-start(bf16[96,1024]{1,0:T(8,128)(2,1)S(1)} %collective-permute-done.16), channel_id=1, source_target_pairs={{384,0},{0,128},{128,256},{256,384},{385,1},{1,129},{129,257},{257... | collective-permute-start | bytes 589832 | tf_op jit(solution)/shard_map/ppermute | solution.py:19
  67.1 3.7 %collective-permute-start.14 = (bf16[64,2048]{1,0:T(8,128)(2,1)S(1)}, bf16[64,2048]{1,0:T(8,128)(2,1)S(1)}, u32[]{:S(2)}, u32[]{:S(2)}) collective-permute-start(bf16[64,2048]{1,0:T(8,128)(2,1)S(1)} %pad_maximum_fusion.2), channel_id=1, source_target_pairs={{4,0},{8,4},{12,8},{0,12},{5,1},{9,5},{13,9},{1,13},{6,2},{10,6},{... | collective-permute-start | bytes 786440 | tf_op jit(solution)/shard_map/ppermute | solution.py:19
  70.8 3.1 %collective-permute-start.15 = (bf16[64,2048]{1,0:T(8,128)(2,1)S(1)}, bf16[64,2048]{1,0:T(8,128)(2,1)S(1)}, u32[]{:S(2)}, u32[]{:S(2)}) collective-permute-start(bf16[64,2048]{1,0:T(8,128)(2,1)S(1)} %pad_maximum_fusion.2), channel_id=1, source_target_pairs={{8,0},{12,4},{0,8},{4,12},{9,1},{13,5},{1,9},{5,13},{10,2},{14,6},... | collective-permute-start | bytes 786440 | tf_op jit(solution)/shard_map/ppermute | solution.py:19
  76.5 4.3 %collective-permute-start.7 = (bf16[96,3584]{1,0:T(8,128)(2,1)S(1)}, bf16[96,3584]{1,0:T(8,128)(2,1)S(1)}, u32[]{:S(2)}, u32[]{:S(2)}) collective-permute-start(bf16[96,3584]{1,0:T(8,128)(2,1)S(1)} %collective-permute-done.6), channel_id=1, source_target_pairs={{128,0},{256,128},{384,256},{0,384},{129,1},{257,129},{385,257},{1... | collective-permute-start | bytes 2064392 | tf_op jit(solution)/shard_map/ppermute | solution.py:19
  80.8 3.4 %collective-permute-start.8 = (bf16[96,3584]{1,0:T(8,128)(2,1)S(1)}, bf16[96,3584]{1,0:T(8,128)(2,1)S(1)}, u32[]{:S(2)}, u32[]{:S(2)}) collective-permute-start(bf16[96,3584]{1,0:T(8,128)(2,1)S(1)} %collective-permute-done.6), channel_id=1, source_target_pairs={{256,0},{384,128},{0,256},{128,384},{257,1},{385,129},{1,257},{129... | collective-permute-start | bytes 2064392 | tf_op jit(solution)/shard_map/ppermute | solution.py:19
  84.3 24.7 %collective-permute-done.7 = bf16[96,3584]{1,0:T(8,128)(2,1)S(1)} collective-permute-done((bf16[96,3584]{1,0:T(8,128)(2,1)S(1)}, bf16[96,3584]{1,0:T(8,128)(2,1)S(1)}, u32[]{:S(2)}, u32[]{:S(2)}) %collective-permute-start.7) | collective-permute-done | bytes 688160 | tf_op jit(solution)/shard_map/ppermute | solution.py:19
  113.0 10.5 %collective-permute-done.9 = bf16[96,3584]{1,0:T(8,128)(2,1)S(1)} collective-permute-done((bf16[96,3584]{1,0:T(8,128)(2,1)S(1)}, bf16[96,3584]{1,0:T(8,128)(2,1)S(1)}, u32[]{:S(2)}, u32[]{:S(2)}) %collective-permute-start.9) | collective-permute-done | bytes 688160 | tf_op jit(solution)/shard_map/ppermute | solution.py:19
  125.6 4.1 %collective-permute-start.3 = (bf16[64,7168]{1,0:T(8,128)(2,1)S(1)}, bf16[64,7168]{1,0:T(8,128)(2,1)S(1)}, u32[]{:S(2)}, u32[]{:S(2)}) collective-permute-start(bf16[64,7168]{1,0:T(8,128)(2,1)S(1)} %pad_maximum_fusion), channel_id=1, source_target_pairs={{12,0},{0,4},{4,8},{8,12},{13,1},{1,5},{5,9},{9,13},{14,2},{2,6},{... | collective-permute-start | bytes 2752520 | tf_op jit(solution)/shard_map/ppermute | solution.py:19
  131.7 4.0 %collective-permute-start.5 = (bf16[64,7168]{1,0:T(8,128)(2,1)S(1)}, bf16[64,7168]{1,0:T(8,128)(2,1)S(1)}, u32[]{:S(2)}, u32[]{:S(2)}) collective-permute-start(bf16[64,7168]{1,0:T(8,128)(2,1)S(1)} %pad_maximum_fusion), channel_id=1, source_target_pairs={{8,0},{12,4},{0,8},{4,12},{9,1},{13,5},{1,9},{5,13},{10,2},{14,6},... | collective-permute-start | bytes 2752520 | tf_op jit(solution)/shard_map/ppermute | solution.py:19
  135.8 33.9 %collective-permute-done.3 = bf16[64,7168]{1,0:T(8,128)(2,1)S(1)} collective-permute-done((bf16[64,7168]{1,0:T(8,128)(2,1)S(1)}, bf16[64,7168]{1,0:T(8,128)(2,1)S(1)}, u32[]{:S(2)}, u32[]{:S(2)}) %collective-permute-start.3) | collective-permute-done | bytes 917536 | tf_op jit(solution)/shard_map/ppermute | solution.py:19
  169.7 5.3 %collective-permute-done.4 = bf16[64,7168]{1,0:T(8,128)(2,1)S(1)} collective-permute-done((bf16[64,7168]{1,0:T(8,128)(2,1)S(1)}, bf16[64,7168]{1,0:T(8,128)(2,1)S(1)}, u32[]{:S(2)}, u32[]{:S(2)}) %collective-permute-start.4) | collective-permute-done | bytes 917536 | tf_op jit(solution)/shard_map/ppermute | solution.py:19
  176.6 11.1 %collective-permute-start.21 = (s16[272,768]{1,0:T(8,128)(2,1)S(1)}, s16[272,768]{1,0:T(8,128)(2,1)S(1)}, u32[]{:S(2)}, u32[]{:S(2)}) collective-permute-start(s16[272,768]{1,0:T(8,128)(2,1)S(1)} %pad_add_fusion), channel_id=1, source_target_pairs={{0,2},{2,0},{1,3},{3,1},{4,6},{6,4},{5,7},{7,5},{8,10},{10,8},{9,1... | collective-permute-start | bytes 1253384 | tf_op jit(solution)/shard_map/ppermute | solution.py:27
  187.8 37.4 %collective-permute-done.21 = s16[272,768]{1,0:T(8,128)(2,1)S(1)} collective-permute-done((s16[272,768]{1,0:T(8,128)(2,1)S(1)}, s16[272,768]{1,0:T(8,128)(2,1)S(1)}, u32[]{:S(2)}, u32[]{:S(2)}) %collective-permute-start.21) | collective-permute-done | bytes 417824 | tf_op jit(solution)/shard_map/ppermute | solution.py:27
  234.8 3.0 %collective-permute-done.23 = f32[2,16,96]{2,0,1:T(2,128)S(1)} collective-permute-done((f32[2,16,96]{2,0,1:T(2,128)S(1)}, f32[2,16,96]{2,0,1:T(2,128)S(1)}, u32[]{:S(2)}, u32[]{:S(2)}) %collective-permute-start.23) | collective-permute-done | bytes 12320 | tf_op jit(solution)/shard_map/ppermute | solution.py:27
  237.9 8.4 %collective-permute-start.24 = (f32[2,16,96]{2,1,0:T(8,128)S(1)}, f32[2,16,96]{2,1,0:T(8,128)S(1)}, u32[]{:S(2)}, u32[]{:S(2)}) collective-permute-start(f32[2,16,96]{2,1,0:T(8,128)S(1)} %bitcast.39), channel_id=1, source_target_pairs={{0,2},{2,0},{1,3},{3,1},{4,6},{6,4},{5,7},{7,5},{8,10},{10,8},{9,1... | collective-permute-start | bytes 36872 | tf_op jit(solution)/shard_map/ppermute | solution.py:27
  246.4 5.9 %collective-permute-done.24 = f32[2,16,96]{2,1,0:T(8,128)S(1)} collective-permute-done((f32[2,16,96]{2,1,0:T(8,128)S(1)}, f32[2,16,96]{2,1,0:T(8,128)S(1)}, u32[]{:S(2)}, u32[]{:S(2)}) %collective-permute-start.24) | collective-permute-done | bytes 12320 | tf_op jit(solution)/shard_map/ppermute | solution.py:27
  (86 shorter events, 36.9 us)
Async XLA Ops:
  1.8 13.6 %collective-permute-start = (bf16[16,4608]{1,0:T(8,128)(2,1)S(1)}, bf16[16,4608]{1,0:T(8,128)(2,1)S(1)}, u32[]{:S(2)}, u32[]{:S(2)}) collective-permute-start(bf16[16,4608]{1,0:T(8,128)(2,1)S(1)} %constant_dynamic-slice_fusion.2), channel_id=1, source_target_pairs={{0,1},{1,0},{2,3},{3,2},{4,5},{5,4},{6,7},{7,6},{8,9},{9,8},{10,11... | collective-permute-start | bytes 442376 | tf_op jit(solution)/shard_map/ppermute | solution.py:27
  5.0 71.5 %collective-permute-start.6 = (bf16[96,3584]{1,0:T(8,128)(2,1)S(1)}, bf16[96,3584]{1,0:T(8,128)(2,1)S(1)}, u32[]{:S(2)}, u32[]{:S(2)}) collective-permute-start(bf16[96,3584]{1,0:T(8,128)(2,1)S(1)} %constant_dynamic-slice_fusion.1), channel_id=1, source_target_pairs={{0,16},{16,0},{1,17},{17,1},{2,18},{18,2},{3,19},{19,3},{4,20},{20... | collective-permute-start | bytes 2064392 | tf_op jit(solution)/shard_map/ppermute | solution.py:27
  8.0 21.5 %collective-permute-start.16 = (bf16[96,1024]{1,0:T(8,128)(2,1)S(1)}, bf16[96,1024]{1,0:T(8,128)(2,1)S(1)}, u32[]{:S(2)}, u32[]{:S(2)}) collective-permute-start(bf16[96,1024]{1,0:T(8,128)(2,1)S(1)} %constant_dynamic-slice_fusion), channel_id=1, source_target_pairs={{0,16},{16,0},{1,17},{17,1},{2,18},{18,2},{3,19},{19,3},{4,20},{20... | collective-permute-start | bytes 589832 | tf_op jit(solution)/shard_map/ppermute | solution.py:27
  15.5 49.4 %collective-permute-start.1 = (bf16[16,7168]{1,0:T(8,128)(2,1)S(1)}, bf16[16,7168]{1,0:T(8,128)(2,1)S(1)}, u32[]{:S(2)}, u32[]{:S(2)}) collective-permute-start(bf16[16,7168]{1,0:T(8,128)(2,1)S(1)} %get-tuple-element.5), channel_id=1, source_target_pairs={{0,64},{32,96},{64,0},{96,32},{1,65},{33,97},{65,1},{97,33},{2,66}... | collective-permute-start | bytes 688136 | tf_op jit(solution)/shard_map/ppermute | solution.py:23
  24.9 28.5 %collective-permute-start.11 = (bf16[16,2048]{1,0:T(8,128)(2,1)S(1)}, bf16[16,2048]{1,0:T(8,128)(2,1)S(1)}, u32[]{:S(2)}, u32[]{:S(2)}) collective-permute-start(bf16[16,2048]{1,0:T(8,128)(2,1)S(1)} %get-tuple-element.11), channel_id=1, source_target_pairs={{0,64},{32,96},{64,0},{96,32},{1,65},{33,97},{65,1},{97,33},{2,66}... | collective-permute-start | bytes 196616 | tf_op jit(solution)/shard_map/ppermute | solution.py:23
  29.5 37.5 %collective-permute-start.17 = (bf16[96,1024]{1,0:T(8,128)(2,1)S(1)}, bf16[96,1024]{1,0:T(8,128)(2,1)S(1)}, u32[]{:S(2)}, u32[]{:S(2)}) collective-permute-start(bf16[96,1024]{1,0:T(8,128)(2,1)S(1)} %collective-permute-done.16), channel_id=1, source_target_pairs={{128,0},{256,128},{384,256},{0,384},{129,1},{257,129},{385,257},{1... | collective-permute-start | bytes 589832 | tf_op jit(solution)/shard_map/ppermute | solution.py:19
  34.2 36.6 %collective-permute-start.18 = (bf16[96,1024]{1,0:T(8,128)(2,1)S(1)}, bf16[96,1024]{1,0:T(8,128)(2,1)S(1)}, u32[]{:S(2)}, u32[]{:S(2)}) collective-permute-start(bf16[96,1024]{1,0:T(8,128)(2,1)S(1)} %collective-permute-done.16), channel_id=1, source_target_pairs={{256,0},{384,128},{0,256},{128,384},{257,1},{385,129},{1,257},{129... | collective-permute-start | bytes 589832 | tf_op jit(solution)/shard_map/ppermute | solution.py:19
  53.4 8.0 %collective-permute-start.12 = (bf16[32,2048]{1,0:T(8,128)(2,1)S(1)}, bf16[32,2048]{1,0:T(8,128)(2,1)S(1)}, u32[]{:S(2)}, u32[]{:S(2)}) collective-permute-start(bf16[32,2048]{1,0:T(8,128)(2,1)S(1)} %pad_maximum_fusion.4), channel_id=1, source_target_pairs={{0,32},{32,0},{64,96},{96,64},{1,33},{33,1},{65,97},{97,65},{2,34}... | collective-permute-start | bytes 393224 | tf_op jit(solution)/shard_map/ppermute | solution.py:23
  61.4 12.6 %collective-permute-start.19 = (bf16[96,1024]{1,0:T(8,128)(2,1)S(1)}, bf16[96,1024]{1,0:T(8,128)(2,1)S(1)}, u32[]{:S(2)}, u32[]{:S(2)}) collective-permute-start(bf16[96,1024]{1,0:T(8,128)(2,1)S(1)} %collective-permute-done.16), channel_id=1, source_target_pairs={{384,0},{0,128},{128,256},{256,384},{385,1},{1,129},{129,257},{257... | collective-permute-start | bytes 589832 | tf_op jit(solution)/shard_map/ppermute | solution.py:19
  64.8 16.0 %collective-permute-start.13 = (bf16[64,2048]{1,0:T(8,128)(2,1)S(1)}, bf16[64,2048]{1,0:T(8,128)(2,1)S(1)}, u32[]{:S(2)}, u32[]{:S(2)}) collective-permute-start(bf16[64,2048]{1,0:T(8,128)(2,1)S(1)} %pad_maximum_fusion.2), channel_id=1, source_target_pairs={{12,0},{0,4},{4,8},{8,12},{13,1},{1,5},{5,9},{9,13},{14,2},{2,6},{... | collective-permute-start | bytes 786440 | tf_op jit(solution)/shard_map/ppermute | solution.py:19
  67.1 58.4 %collective-permute-start.14 = (bf16[64,2048]{1,0:T(8,128)(2,1)S(1)}, bf16[64,2048]{1,0:T(8,128)(2,1)S(1)}, u32[]{:S(2)}, u32[]{:S(2)}) collective-permute-start(bf16[64,2048]{1,0:T(8,128)(2,1)S(1)} %pad_maximum_fusion.2), channel_id=1, source_target_pairs={{4,0},{8,4},{12,8},{0,12},{5,1},{9,5},{13,9},{1,13},{6,2},{10,6},{... | collective-permute-start | bytes 786440 | tf_op jit(solution)/shard_map/ppermute | solution.py:19
  70.8 58.9 %collective-permute-start.15 = (bf16[64,2048]{1,0:T(8,128)(2,1)S(1)}, bf16[64,2048]{1,0:T(8,128)(2,1)S(1)}, u32[]{:S(2)}, u32[]{:S(2)}) collective-permute-start(bf16[64,2048]{1,0:T(8,128)(2,1)S(1)} %pad_maximum_fusion.2), channel_id=1, source_target_pairs={{8,0},{12,4},{0,8},{4,12},{9,1},{13,5},{1,9},{5,13},{10,2},{14,6},... | collective-permute-start | bytes 786440 | tf_op jit(solution)/shard_map/ppermute | solution.py:19
  74.0 51.5 %collective-permute-start.2 = (bf16[32,7168]{1,0:T(8,128)(2,1)S(1)}, bf16[32,7168]{1,0:T(8,128)(2,1)S(1)}, u32[]{:S(2)}, u32[]{:S(2)}) collective-permute-start(bf16[32,7168]{1,0:T(8,128)(2,1)S(1)} %pad_maximum_fusion.1), channel_id=1, source_target_pairs={{0,32},{32,0},{64,96},{96,64},{1,33},{33,1},{65,97},{97,65},{2,34}... | collective-permute-start | bytes 1376264 | tf_op jit(solution)/shard_map/ppermute | solution.py:23
  76.5 32.5 %collective-permute-start.7 = (bf16[96,3584]{1,0:T(8,128)(2,1)S(1)}, bf16[96,3584]{1,0:T(8,128)(2,1)S(1)}, u32[]{:S(2)}, u32[]{:S(2)}) collective-permute-start(bf16[96,3584]{1,0:T(8,128)(2,1)S(1)} %collective-permute-done.6), channel_id=1, source_target_pairs={{128,0},{256,128},{384,256},{0,384},{129,1},{257,129},{385,257},{1... | collective-permute-start | bytes 2064392 | tf_op jit(solution)/shard_map/ppermute | solution.py:19
  80.8 30.2 %collective-permute-start.8 = (bf16[96,3584]{1,0:T(8,128)(2,1)S(1)}, bf16[96,3584]{1,0:T(8,128)(2,1)S(1)}, u32[]{:S(2)}, u32[]{:S(2)}) collective-permute-start(bf16[96,3584]{1,0:T(8,128)(2,1)S(1)} %collective-permute-done.6), channel_id=1, source_target_pairs={{256,0},{384,128},{0,256},{128,384},{257,1},{385,129},{1,257},{129... | collective-permute-start | bytes 2064392 | tf_op jit(solution)/shard_map/ppermute | solution.py:19
  109.0 14.5 %collective-permute-start.9 = (bf16[96,3584]{1,0:T(8,128)(2,1)S(1)}, bf16[96,3584]{1,0:T(8,128)(2,1)S(1)}, u32[]{:S(2)}, u32[]{:S(2)}) collective-permute-start(bf16[96,3584]{1,0:T(8,128)(2,1)S(1)} %collective-permute-done.6), channel_id=1, source_target_pairs={{384,0},{0,128},{128,256},{256,384},{385,1},{1,129},{129,257},{257... | collective-permute-start | bytes 2064392 | tf_op jit(solution)/shard_map/ppermute | solution.py:19
  111.0 64.0 %collective-permute-start.20 = (bf16[768,1024]{1,0:T(8,128)(2,1)S(1)}, bf16[768,1024]{1,0:T(8,128)(2,1)S(1)}, u32[]{:S(2)}, u32[]{:S(2)}) collective-permute-start(bf16[768,1024]{1,0:T(8,128)(2,1)S(1)} %constant_dynamic-update-slice_fusion.19), channel_id=1, source_target_pairs={{0,1},{1,0},{2,3},{3,2},{4,5},{5,4},{6,7},{7,6},{8,9},{9,8},{10,11... | collective-permute-start | bytes 4718600 | tf_op jit(solution)/shard_map/ppermute | solution.py:27
  123.6 101.8 %collective-permute-start.10 = (bf16[768,3584]{1,0:T(8,128)(2,1)S(1)}, bf16[768,3584]{1,0:T(8,128)(2,1)S(1)}, u32[]{:S(2)}, u32[]{:S(2)}) collective-permute-start(bf16[768,3584]{1,0:T(8,128)(2,1)S(1)} %constant_dynamic-update-slice_fusion.8), channel_id=1, source_target_pairs={{0,1},{1,0},{2,3},{3,2},{4,5},{5,4},{6,7},{7,6},{8,9},{9,8},{10,11... | collective-permute-start | bytes 16515080 | tf_op jit(solution)/shard_map/ppermute | solution.py:27
  125.6 44.0 %collective-permute-start.3 = (bf16[64,7168]{1,0:T(8,128)(2,1)S(1)}, bf16[64,7168]{1,0:T(8,128)(2,1)S(1)}, u32[]{:S(2)}, u32[]{:S(2)}) collective-permute-start(bf16[64,7168]{1,0:T(8,128)(2,1)S(1)} %pad_maximum_fusion), channel_id=1, source_target_pairs={{12,0},{0,4},{4,8},{8,12},{13,1},{1,5},{5,9},{9,13},{14,2},{2,6},{... | collective-permute-start | bytes 2752520 | tf_op jit(solution)/shard_map/ppermute | solution.py:19
  129.7 45.2 %collective-permute-start.4 = (bf16[64,7168]{1,0:T(8,128)(2,1)S(1)}, bf16[64,7168]{1,0:T(8,128)(2,1)S(1)}, u32[]{:S(2)}, u32[]{:S(2)}) collective-permute-start(bf16[64,7168]{1,0:T(8,128)(2,1)S(1)} %pad_maximum_fusion), channel_id=1, source_target_pairs={{4,0},{8,4},{12,8},{0,12},{5,1},{9,5},{13,9},{1,13},{6,2},{10,6},{... | collective-permute-start | bytes 2752520 | tf_op jit(solution)/shard_map/ppermute | solution.py:19
  131.7 56.0 %collective-permute-start.5 = (bf16[64,7168]{1,0:T(8,128)(2,1)S(1)}, bf16[64,7168]{1,0:T(8,128)(2,1)S(1)}, u32[]{:S(2)}, u32[]{:S(2)}) collective-permute-start(bf16[64,7168]{1,0:T(8,128)(2,1)S(1)} %pad_maximum_fusion), channel_id=1, source_target_pairs={{8,0},{12,4},{0,8},{4,12},{9,1},{13,5},{1,9},{5,13},{10,2},{14,6},... | collective-permute-start | bytes 2752520 | tf_op jit(solution)/shard_map/ppermute | solution.py:19
  176.6 48.6 %collective-permute-start.21 = (s16[272,768]{1,0:T(8,128)(2,1)S(1)}, s16[272,768]{1,0:T(8,128)(2,1)S(1)}, u32[]{:S(2)}, u32[]{:S(2)}) collective-permute-start(s16[272,768]{1,0:T(8,128)(2,1)S(1)} %pad_add_fusion), channel_id=1, source_target_pairs={{0,2},{2,0},{1,3},{3,1},{4,6},{6,4},{5,7},{7,5},{8,10},{10,8},{9,1... | collective-permute-start | bytes 1253384 | tf_op jit(solution)/shard_map/ppermute | solution.py:27
  232.1 5.7 %collective-permute-start.23 = (f32[2,16,96]{2,0,1:T(2,128)S(1)}, f32[2,16,96]{2,0,1:T(2,128)S(1)}, u32[]{:S(2)}, u32[]{:S(2)}) collective-permute-start(f32[2,16,96]{2,0,1:T(2,128)S(1)} %get-tuple-element.17), channel_id=1, source_target_pairs={{0,16},{16,0},{1,17},{17,1},{2,18},{18,2},{3,19},{19,3},{4,20},{20... | collective-permute-start | bytes 36872 | tf_op jit(solution)/shard_map/ppermute | solution.py:27
  237.9 14.4 %collective-permute-start.24 = (f32[2,16,96]{2,1,0:T(8,128)S(1)}, f32[2,16,96]{2,1,0:T(8,128)S(1)}, u32[]{:S(2)}, u32[]{:S(2)}) collective-permute-start(f32[2,16,96]{2,1,0:T(8,128)S(1)} %bitcast.39), channel_id=1, source_target_pairs={{0,2},{2,0},{1,3},{3,1},{4,6},{6,4},{5,7},{7,5},{8,10},{10,8},{9,1... | collective-permute-start | bytes 36872 | tf_op jit(solution)/shard_map/ppermute | solution.py:27
  (3 other events, 83.6 us)

commit v2 on v0

v2 whole, which is shorter than its diff:
```python
import jax
import jax.numpy as jnp
from jax import lax
from jax.sharding import Mesh, PartitionSpec as P

RANK = 32
GROUP = 16
SWAP = ((0, 1), (1, 0))
Z_OFFSETS = (0, 4, 2, 6, 1, 5, 3, 7)
TOKENS_BY, FACTORS_BY = 1, 3
Y = ("y_hi", "y_lo")


def rows_of(data_rows, factor_rows):
    return lax.dot_general(factor_rows, data_rows, (((1,), (1,)), ((), ())), preferred_element_type=jnp.float32)


def flip(value, axes, bits):
    return lax.ppermute(value, axes, [(i, i ^ bits) for i in range(lax.axis_size(axes))])


def swap(value, axis):
    return lax.ppermute(value, axis, SWAP)


def grow(block, bits):
    return jnp.concatenate([block, flip(block, "z_lo", bits)], axis=0)


def after(value, done):
    return jnp.where(jnp.isnan(done[0, 0]), jnp.zeros_like(value), value)


def coded_half(partial):
    count, tokens = partial.shape[0] // GROUP, partial.shape[1]
    blocks = partial.reshape(count, GROUP, tokens)
    largest = jnp.max(jnp.abs(blocks), axis=1)
    exponent = jnp.clip(jnp.ceil(jnp.log2(jnp.maximum(largest, 1e-30)) + 0.01), -100.0, 100.0)
    coded = jnp.round(blocks * (jnp.exp2(-exponent) * 32766.0)[:, None, :]).astype(jnp.int16)
    return blocks, jnp.concatenate([coded.reshape(count * GROUP, tokens), exponent.astype(jnp.int16)], axis=0)


def sum_over_halves(blocks, sent):
    count, _, tokens = blocks.shape
    got = swap(sent, "z_half").astype(jnp.float32)
    scale = jnp.exp2(got[count * GROUP :]) * (1.0 / 32766.0)
    return blocks + got[: count * GROUP].reshape(count, GROUP, tokens) * scale[:, None, :]


def scores_of(left, right):
    return (left * right).reshape(-1, RANK, left.shape[1]).sum(axis=1)


def split_sum(near, far, core):
    return jnp.where(core == 0, near, far) + swap(jnp.where(core == 0, far, near), "core")


def body(token_grads, token_inputs, up_factors, in_factors, loss_mask):
    y_at, core, z_half = lax.axis_index(Y), lax.axis_index("core"), lax.axis_index("z_half")
    tokens, quarter = token_grads.shape[0], token_grads.shape[0] // 4

    second = lax.axis_index("y_lo") == 1
    pair_inputs = flip(token_inputs, Y, TOKENS_BY)
    inputs = jnp.where(
        second, jnp.concatenate([pair_inputs, token_inputs], axis=0), jnp.concatenate([token_inputs, pair_inputs], axis=0)
    )
    grads = lax.all_gather(token_grads, "y_lo", axis=0, tiled=True)
    in_near = grow(grow(grow(in_factors, 4), 2), 1)
    in_far = flip(in_near, Y, FACTORS_BY)
    blocks, sent = coded_half(split_sum(rows_of(inputs, in_near), rows_of(inputs, in_far), core))
    right = sum_over_halves(blocks, sent)

    up_near = grow(grow(up_factors, 4), 2)
    next_near = flip(up_near, "z_lo", 1)
    up_far = flip(up_near, Y, FACTORS_BY)
    next_far = flip(next_near, Y, FACTORS_BY)
    right = right.reshape(-1, 2 * tokens)
    other = swap(after(right, up_far[:1, :1] + next_far[:1, :1]), "core")
    right_near, right_far = jnp.where(core == 0, right, other), jnp.where(core == 0, other, right)
    half = right.shape[0] // 2
    left_near, left_far, left_last = lax.optimization_barrier(
        [rows_of(grads, up) for up in (jnp.concatenate([up_near, next_near], axis=0), up_far, next_far)]
    )
    summed = jnp.concatenate(
        [
            scores_of(left_near, right_near),
            scores_of(left_far, right_far[:half]),
            scores_of(left_last, right_far[half:]),
        ],
        axis=0,
    )

    count = summed.shape[0]
    parts = summed.reshape(count, 2, 2, 2, quarter).transpose(2, 3, 1, 0, 4)
    mine = lax.dynamic_index_in_dim(parts, core, 1, keepdims=False)
    mine = mine + swap(lax.dynamic_index_in_dim(parts, 1 - core, 1, keepdims=False), "core")
    own, other = jnp.where(second, mine[:, 1], mine[:, 0]), jnp.where(second, mine[:, 0], mine[:, 1])
    mine = jnp.stack([own, flip(other, Y, TOKENS_BY)], axis=1)
    result = lax.dynamic_index_in_dim(mine, z_half, 0, keepdims=False)
    result = result + swap(lax.dynamic_index_in_dim(mine, 1 - z_half, 0, keepdims=False), "z_half")
    result = result.reshape(2 * count, quarter)

    at = lax.broadcasted_iota(jnp.int32, (2 * count, 2 * count), 0)
    column = lax.broadcasted_iota(jnp.int32, (2 * count, 2 * count), 1)
    z_lo = lax.axis_index("z_lo")
    place = jnp.zeros_like(at)
    for pair in range(2):
        for far in range(2):
            for k, bits in enumerate(Z_OFFSETS):
                row = pair * count + far * len(Z_OFFSETS) + k
                to = (z_lo ^ bits) * 4 + (y_at ^ (pair * TOKENS_BY) ^ (far * FACTORS_BY))
                place = place + jnp.where(at == row, to, 0)
    select = (place == column).astype(jnp.float32)
    scores = lax.dot_general(
        result, select, (((0,), (0,)), ((), ())), precision=lax.Precision.HIGHEST, preferred_element_type=jnp.float32
    )
    share = lax.dynamic_slice_in_dim(loss_mask, (z_half * 2 + core) * quarter, quarter, 0)
    return scores * share.astype(jnp.float32)[:, None]


def solution(mesh):
    split = Mesh(mesh.devices.reshape(4, 8, 2, 2, 2, 2), ("query", "z_lo") + Y + ("z_half", "core"))
    ctx, ffn = ("z_lo",) + Y, ("z_half", "core")
    in_specs = (
        P(ctx, ffn),
        P(ctx, ffn),
        P(("query",) + ctx, ffn),
        P(("query",) + ctx, ffn),
        P(ctx),
    )
    return jax.shard_map(body, mesh=split, in_specs=in_specs, out_specs=P(ctx + ffn, "query"), check_vma=False)
```

time: 740 us -> 198 us (0.27)
  the two profiles are of different devices: /device:TPU:97 before, /device:TPU:132 now
where the time goes in v2:
time: 198 us; the launch traced here: 197 us
  waiting for transfers between devices  89.8 us (45%)
  starting transfers between devices  74.1 us (37%)
  between operations  15.2 us (8%)
  matrix products  13.2 us (7%)
  local copies, waits for them, and re-layouts  2.78 us (1%)
  other arithmetic  2.1 us (1%)
    ppermute x11, starting transfers between devices, flip(): lax.ppermute(value, axes, [(i, i ^ bits) for i in range(lax.axis_size(axe...  50.1 us
    ppermute x11, waiting for transfers between devices, flip(): lax.ppermute(value, axes, [(i, i ^ bits) for i in range(lax.axis_size(axe...  45.2 us
    ppermute x5, waiting for transfers between devices, swap(): return lax.ppermute(value, axis, SWAP)  43.9 us
    ppermute x5, starting transfers between devices, swap(): return lax.ppermute(value, axis, SWAP)  24.1 us
    dot_general x5, matrix products, rows_of(): lax.dot_general(factor_rows, data_rows, (((1,), (1,)), ((), ())), preferr...  12.3 us
  transfers between devices with their start and end apart: 17, of which 10 were waited for; matrix products, arithmetic and copies ran while one was open for 4% of the time, Pallas kernels for 0%

profile of v2, /device:TPU:132, one launch (start us, length us, event | category | flops | bytes accessed | tf_op | source)
XLA Modules:
  0.0 197.2 jit_solution(6233608305859677312)
XLA Ops:
  9.2 7.8 %collective-permute-start.5 = (bf16[32,1024]{1,0:T(8,128)(2,1)}, bf16[32,1024]{1,0:T(8,128)(2,1)S(1)}, u32[]{:S(2)}, u32[]{:S(2)}) collective-permute-start(bf16[32,1024]{1,0:T(8,128)(2,1)} %param.8), channel_id=1, source_target_pairs={{0,64},{16,80},{32,96},{48,112},{64,0},{80,16},{96,32},{112,48},{1... | collective-permute-start | bytes 196616 | tf_op jit(solution)/shard_map/ppermute | solution.py:19
  17.0 3.5 %collective-permute-start.8 = (bf16[384,1024]{1,0:T(8,128)(2,1)}, bf16[384,1024]{1,0:T(8,128)(2,1)}, u32[]{:S(2)}, u32[]{:S(2)}) collective-permute-start(bf16[384,1024]{1,0:T(8,128)(2,1)} %param.6), channel_id=1, source_target_pairs={{0,4},{4,0},{8,12},{12,8},{1,5},{5,1},{9,13},{13,9},{2,6},{6,2},{1... | collective-permute-start | bytes 2359304 | tf_op jit(solution)/shard_map/ppermute | solution.py:19
  21.5 13.5 %collective-permute-done.5 = bf16[32,1024]{1,0:T(8,128)(2,1)S(1)} collective-permute-done((bf16[32,1024]{1,0:T(8,128)(2,1)}, bf16[32,1024]{1,0:T(8,128)(2,1)S(1)}, u32[]{:S(2)}, u32[]{:S(2)}) %collective-permute-start.5) | collective-permute-done | bytes 65568 | tf_op jit(solution)/shard_map/ppermute | solution.py:19
  35.0 4.0 %collective-permute-start.6 = (bf16[64,1024]{1,0:T(8,128)(2,1)S(1)}, bf16[64,1024]{1,0:T(8,128)(2,1)S(1)}, u32[]{:S(2)}, u32[]{:S(2)}) collective-permute-start(bf16[64,1024]{1,0:T(8,128)(2,1)S(1)} %pad_maximum_fusion.2), channel_id=1, source_target_pairs={{0,32},{16,48},{32,0},{48,16},{64,96},{80,112},{96,64},{112,80},{1... | collective-permute-start | bytes 393224 | tf_op jit(solution)/shard_map/ppermute | solution.py:19
  39.1 3.7 %collective-permute-done.6 = bf16[64,1024]{1,0:T(8,128)(2,1)S(1)} collective-permute-done((bf16[64,1024]{1,0:T(8,128)(2,1)S(1)}, bf16[64,1024]{1,0:T(8,128)(2,1)S(1)}, u32[]{:S(2)}, u32[]{:S(2)}) %collective-permute-start.6) | collective-permute-done | bytes 131104 | tf_op jit(solution)/shard_map/ppermute | solution.py:19
  42.8 9.5 %collective-permute-start.7 = (bf16[128,1024]{1,0:T(8,128)(2,1)S(1)}, bf16[128,1024]{1,0:T(8,128)(2,1)S(1)}, u32[]{:S(2)}, u32[]{:S(2)}) collective-permute-start(bf16[128,1024]{1,0:T(8,128)(2,1)S(1)} %pad_maximum_fusion.1), channel_id=1, source_target_pairs={{0,16},{16,0},{32,48},{48,32},{64,80},{80,64},{96,112},{112,96},{1... | collective-permute-start | bytes 786440 | tf_op jit(solution)/shard_map/ppermute | solution.py:19
  52.4 4.5 %collective-permute-start.1 = (bf16[64,3584]{1,0:T(8,128)(2,1)S(1)}, bf16[64,3584]{1,0:T(8,128)(2,1)S(1)}, u32[]{:S(2)}, u32[]{:S(2)}) collective-permute-start(bf16[64,3584]{1,0:T(8,128)(2,1)S(1)} %pad_maximum_fusion), channel_id=1, source_target_pairs={{0,32},{16,48},{32,0},{48,16},{64,96},{80,112},{96,64},{112,80},{1... | collective-permute-start | bytes 1376264 | tf_op jit(solution)/shard_map/ppermute | solution.py:19
  57.0 3.7 %collective-permute-done.7 = bf16[128,1024]{1,0:T(8,128)(2,1)S(1)} collective-permute-done((bf16[128,1024]{1,0:T(8,128)(2,1)S(1)}, bf16[128,1024]{1,0:T(8,128)(2,1)S(1)}, u32[]{:S(2)}, u32[]{:S(2)}) %collective-permute-start.7) | collective-permute-done | bytes 262176 | tf_op jit(solution)/shard_map/ppermute | solution.py:19
  60.7 4.9 %collective-permute-start.9 = (bf16[256,1024]{1,0:T(8,128)(2,1)S(1)}, bf16[256,1024]{1,0:T(8,128)(2,1)S(1)}, u32[]{:S(2)}, u32[]{:S(2)}) collective-permute-start(bf16[256,1024]{1,0:T(8,128)(2,1)S(1)} %constant_dynamic-update-slice_fusion.3), channel_id=1, source_target_pairs={{0,12},{4,8},{8,4},{12,0},{1,13},{5,9},{9,5},{13,1},{2,14},{6,10},... | collective-permute-start | bytes 1572872 | tf_op jit(solution)/shard_map/ppermute | solution.py:19
  65.6 11.0 %collective-permute-done.1 = bf16[64,3584]{1,0:T(8,128)(2,1)S(1)} collective-permute-done((bf16[64,3584]{1,0:T(8,128)(2,1)S(1)}, bf16[64,3584]{1,0:T(8,128)(2,1)S(1)}, u32[]{:S(2)}, u32[]{:S(2)}) %collective-permute-start.1) | collective-permute-done | bytes 458784 | tf_op jit(solution)/shard_map/ppermute | solution.py:19
  78.6 2.0 %fusion.12 = f32[256,768]{1,0:T(8,128)S(1)} fusion(bf16[256,1024]{1,0:T(8,128)(2,1)S(1)} %constant_dynamic-update-slice_fusion.3, bf16[384,1024]{1,0:T(8,128)(2,1)S(1)} %copy-done.8, bf16[384,1024]{1,0:T(8,128)(2,1)} %collective-permute-done.8, pred[]{:T(512)S(6)} %eq.236), kind=kOutput, calls=%fused_computation.29 | convolution fusion | flops 409731072 | bytes 2883585 | tf_op jit(solution)/shard_map/dot_general | solution.py:15
  80.6 2.0 %broadcast_select_fusion.2 = (f32[256,768]{1,0:T(8,128)S(1)}, f32[256,768]{1,0:T(8,128)S(1)}) fusion(f32[256,768]{1,0:T(8,128)S(1)} %fusion.12, pred[]{:T(512)S(6)} %eq.237, bf16[256,1024]{1,0:T(8,128)(2,1)S(1)} %collective-permute-done.9, bf16[384,1024]{1,0:T(8,128)(2,1)S(1)} %copy-done.8, bf16[384,1024]{1,0:T(8,128)(2,1)} %collective-permute-done.8, ...), kind=kOutput, calls=%fused_computation.27 | convolution fusion | flops 409927680 | bytes 4456450 | tf_op jit(solution)/shard_map/dot_general | solution.py:15
  84.6 4.9 %collective-permute-start.3 = (bf16[128,3584]{1,0:T(8,128)(2,1)S(1)}, bf16[128,3584]{1,0:T(8,128)(2,1)S(1)}, u32[]{:S(2)}, u32[]{:S(2)}) collective-permute-start(bf16[128,3584]{1,0:T(8,128)(2,1)S(1)} %constant_dynamic-update-slice_fusion), channel_id=1, source_target_pairs={{0,12},{4,8},{8,4},{12,0},{1,13},{5,9},{9,5},{13,1},{2,14},{6,10},... | collective-permute-start | bytes 2752520 | tf_op jit(solution)/shard_map/ppermute | solution.py:19
  89.5 9.8 %collective-permute-done.2 = bf16[128,3584]{1,0:T(8,128)(2,1)S(1)} collective-permute-done((bf16[128,3584]{1,0:T(8,128)(2,1)S(1)}, bf16[128,3584]{1,0:T(8,128)(2,1)S(1)}, u32[]{:S(2)}, u32[]{:S(2)}) %collective-permute-start.2) | collective-permute-done | bytes 917536 | tf_op jit(solution)/shard_map/ppermute | solution.py:19
  99.3 4.9 %collective-permute-start.4 = (bf16[128,3584]{1,0:T(8,128)(2,1)S(1)}, bf16[128,3584]{1,0:T(8,128)(2,1)S(1)}, u32[]{:S(2)}, u32[]{:S(2)}) collective-permute-start(bf16[128,3584]{1,0:T(8,128)(2,1)S(1)} %collective-permute-done.2), channel_id=1, source_target_pairs={{0,12},{4,8},{8,4},{12,0},{1,13},{5,9},{9,5},{13,1},{2,14},{6,10},... | collective-permute-start | bytes 2752520 | tf_op jit(solution)/shard_map/ppermute | solution.py:19
  104.6 8.9 %collective-permute-start.11 = (s16[272,768]{1,0:T(8,128)(2,1)S(1)}, s16[272,768]{1,0:T(8,128)(2,1)S(1)}, u32[]{:S(2)}, u32[]{:S(2)}) collective-permute-start(s16[272,768]{1,0:T(8,128)(2,1)S(1)} %pad_add_fusion), channel_id=1, source_target_pairs={{0,2},{2,0},{1,3},{3,1},{4,6},{6,4},{5,7},{7,5},{8,10},{10,8},{9,1... | collective-permute-start | bytes 1253384 | tf_op jit(solution)/shard_map/ppermute | solution.py:23
  114.5 36.4 %collective-permute-done.11 = s16[272,768]{1,0:T(8,128)(2,1)S(1)} collective-permute-done((s16[272,768]{1,0:T(8,128)(2,1)S(1)}, s16[272,768]{1,0:T(8,128)(2,1)S(1)}, u32[]{:S(2)}, u32[]{:S(2)}) %collective-permute-start.11) | collective-permute-done | bytes 417824 | tf_op jit(solution)/shard_map/ppermute | solution.py:23
  155.0 2.2 %collective-permute-done.12 = f32[256,768]{1,0:T(8,128)S(1)} collective-permute-done((f32[256,768]{1,0:T(8,128)S(1)}, f32[256,768]{1,0:T(8,128)S(1)}, u32[]{:S(2)}, u32[]{:S(2)}) %collective-permute-start.12) | collective-permute-done | bytes 786464 | tf_op jit(solution)/shard_map/ppermute | solution.py:23
  157.3 4.6 %fusion = f32[256,768]{1,0:T(8,128)S(1)} fusion(bf16[768,3584]{1,0:T(8,128)(2,1)} %all-gather.2.cloned.1.call-done, bf16[128,3584]{1,0:T(8,128)(2,1)} %copy-done.7, bf16[64,3584]{1,0:T(8,128)(2,1)S(1)} %collective-permute-done.1, bf16[32,3584]{1,0:T(8,128)(2,1)S(1)} %collective-permute-done, bf16[32,3584]{1,0:T(8,128)(2,1)S(1)} %copy-done.1), kind=kOutput, calls=%fused_computation | convolution fusion | flops 1416626176 | bytes 8126464 | tf_op jit(solution)/shard_map/dot_general | solution.py:15
  166.3 2.0 %collective-permute-start.13 = (f32[2,2,16,96]{3,0,1,2:T(2,128)S(1)}, f32[2,2,16,96]{3,0,1,2:T(2,128)S(1)}, u32[]{:S(2)}, u32[]{:S(2)}) collective-permute-start(f32[2,2,16,96]{3,0,1,2:T(2,128)S(1)} %bitcast.52), channel_id=1, source_target_pairs={{0,1},{1,0},{2,3},{3,2},{4,5},{5,4},{6,7},{7,6},{8,9},{9,8},{10,11... | collective-permute-start | bytes 73736 | tf_op jit(solution)/shard_map/ppermute | solution.py:23
  169.4 2.0 %collective-permute-start.14 = (f32[2,16,96]{2,0,1:T(2,128)S(1)}, f32[2,16,96]{2,0,1:T(2,128)S(1)}, u32[]{:S(2)}, u32[]{:S(2)}) collective-permute-start(f32[2,16,96]{2,0,1:T(2,128)S(1)} %fusion.16), channel_id=1, source_target_pairs={{0,4},{4,0},{8,12},{12,8},{1,5},{5,1},{9,13},{13,9},{2,6},{6,2},{1... | collective-permute-start | bytes 36872 | tf_op jit(solution)/shard_map/ppermute | solution.py:19
  171.5 3.6 %collective-permute-done.14 = f32[2,16,96]{2,0,1:T(2,128)S(1)} collective-permute-done((f32[2,16,96]{2,0,1:T(2,128)S(1)}, f32[2,16,96]{2,0,1:T(2,128)S(1)}, u32[]{:S(2)}, u32[]{:S(2)}) %collective-permute-start.14) | collective-permute-done | bytes 12320 | tf_op jit(solution)/shard_map/ppermute | solution.py:19
  175.1 9.3 %collective-permute-start.15 = (f32[2,16,96]{2,1,0:T(8,128)S(1)}, f32[2,16,96]{2,1,0:T(8,128)S(1)}, u32[]{:S(2)}, u32[]{:S(2)}) collective-permute-start(f32[2,16,96]{2,1,0:T(8,128)S(1)} %bitcast.54), channel_id=1, source_target_pairs={{0,2},{2,0},{1,3},{3,1},{4,6},{6,4},{5,7},{7,5},{8,10},{10,8},{9,1... | collective-permute-start | bytes 36872 | tf_op jit(solution)/shard_map/ppermute | solution.py:23
  184.5 5.0 %collective-permute-done.15 = f32[2,16,96]{2,1,0:T(8,128)S(1)} collective-permute-done((f32[2,16,96]{2,1,0:T(8,128)S(1)}, f32[2,16,96]{2,1,0:T(8,128)S(1)}, u32[]{:S(2)}, u32[]{:S(2)}) %collective-permute-start.15) | collective-permute-done | bytes 12320 | tf_op jit(solution)/shard_map/ppermute | solution.py:23
  (67 shorter events, 18.2 us)
Async XLA Ops:
  6.5 45.8 %copy-start.1 = (bf16[32,3584]{1,0:T(8,128)(2,1)S(1)}, bf16[32,3584]{1,0:T(8,128)(2,1)}, u32[]{:S(2)}) copy-start(bf16[32,3584]{1,0:T(8,128)(2,1)} %param.7) | copy-start | bytes 688132
  6.5 28.5 %copy-start.6 = (bf16[32,1024]{1,0:T(8,128)(2,1)S(1)}, bf16[32,1024]{1,0:T(8,128)(2,1)}, u32[]{:S(2)}) copy-start(bf16[32,1024]{1,0:T(8,128)(2,1)} %param.8) | copy-start | bytes 196612
  6.5 72.0 %copy-start.8 = (bf16[384,1024]{1,0:T(8,128)(2,1)S(1)}, bf16[384,1024]{1,0:T(8,128)(2,1)}, u32[]{:S(2)}) copy-start(bf16[384,1024]{1,0:T(8,128)(2,1)} %param.6) | copy-start | bytes 2359300
  6.5 150.8 %all-gather.2.cloned.1.call-start = ((), (), s32[]{:S(2)}) async-start(), calls=%async_computation | async-start | bytes 8257536 | tf_op jit(solution)/shard_map/all_gather | solution.py:67
  7.3 45.1 %collective-permute-start = (bf16[32,3584]{1,0:T(8,128)(2,1)}, bf16[32,3584]{1,0:T(8,128)(2,1)S(1)}, u32[]{:S(2)}, u32[]{:S(2)}) collective-permute-start(bf16[32,3584]{1,0:T(8,128)(2,1)} %param.7), channel_id=1, source_target_pairs={{0,64},{16,80},{32,96},{48,112},{64,0},{80,16},{96,32},{112,48},{1... | collective-permute-start | bytes 688136 | tf_op jit(solution)/shard_map/ppermute | solution.py:19
  9.2 25.8 %collective-permute-start.5 = (bf16[32,1024]{1,0:T(8,128)(2,1)}, bf16[32,1024]{1,0:T(8,128)(2,1)S(1)}, u32[]{:S(2)}, u32[]{:S(2)}) collective-permute-start(bf16[32,1024]{1,0:T(8,128)(2,1)} %param.8), channel_id=1, source_target_pairs={{0,64},{16,80},{32,96},{48,112},{64,0},{80,16},{96,32},{112,48},{1... | collective-permute-start | bytes 196616 | tf_op jit(solution)/shard_map/ppermute | solution.py:19
  17.0 61.6 %collective-permute-start.8 = (bf16[384,1024]{1,0:T(8,128)(2,1)}, bf16[384,1024]{1,0:T(8,128)(2,1)}, u32[]{:S(2)}, u32[]{:S(2)}) collective-permute-start(bf16[384,1024]{1,0:T(8,128)(2,1)} %param.6), channel_id=1, source_target_pairs={{0,4},{4,0},{8,12},{12,8},{1,5},{5,1},{9,13},{13,9},{2,6},{6,2},{1... | collective-permute-start | bytes 2359304 | tf_op jit(solution)/shard_map/ppermute | solution.py:19
  35.0 7.8 %collective-permute-start.6 = (bf16[64,1024]{1,0:T(8,128)(2,1)S(1)}, bf16[64,1024]{1,0:T(8,128)(2,1)S(1)}, u32[]{:S(2)}, u32[]{:S(2)}) collective-permute-start(bf16[64,1024]{1,0:T(8,128)(2,1)S(1)} %pad_maximum_fusion.2), channel_id=1, source_target_pairs={{0,32},{16,48},{32,0},{48,16},{64,96},{80,112},{96,64},{112,80},{1... | collective-permute-start | bytes 393224 | tf_op jit(solution)/shard_map/ppermute | solution.py:19
  42.8 17.9 %collective-permute-start.7 = (bf16[128,1024]{1,0:T(8,128)(2,1)S(1)}, bf16[128,1024]{1,0:T(8,128)(2,1)S(1)}, u32[]{:S(2)}, u32[]{:S(2)}) collective-permute-start(bf16[128,1024]{1,0:T(8,128)(2,1)S(1)} %pad_maximum_fusion.1), channel_id=1, source_target_pairs={{0,16},{16,0},{32,48},{48,32},{64,80},{80,64},{96,112},{112,96},{1... | collective-permute-start | bytes 786440 | tf_op jit(solution)/shard_map/ppermute | solution.py:19
  52.4 24.2 %collective-permute-start.1 = (bf16[64,3584]{1,0:T(8,128)(2,1)S(1)}, bf16[64,3584]{1,0:T(8,128)(2,1)S(1)}, u32[]{:S(2)}, u32[]{:S(2)}) collective-permute-start(bf16[64,3584]{1,0:T(8,128)(2,1)S(1)} %pad_maximum_fusion), channel_id=1, source_target_pairs={{0,32},{16,48},{32,0},{48,16},{64,96},{80,112},{96,64},{112,80},{1... | collective-permute-start | bytes 1376264 | tf_op jit(solution)/shard_map/ppermute | solution.py:19
  60.7 19.9 %collective-permute-start.9 = (bf16[256,1024]{1,0:T(8,128)(2,1)S(1)}, bf16[256,1024]{1,0:T(8,128)(2,1)S(1)}, u32[]{:S(2)}, u32[]{:S(2)}) collective-permute-start(bf16[256,1024]{1,0:T(8,128)(2,1)S(1)} %constant_dynamic-update-slice_fusion.3), channel_id=1, source_target_pairs={{0,12},{4,8},{8,4},{12,0},{1,13},{5,9},{9,5},{13,1},{2,14},{6,10},... | collective-permute-start | bytes 1572872 | tf_op jit(solution)/shard_map/ppermute | solution.py:19
  76.6 22.6 %collective-permute-start.2 = (bf16[128,3584]{1,0:T(8,128)(2,1)S(1)}, bf16[128,3584]{1,0:T(8,128)(2,1)S(1)}, u32[]{:S(2)}, u32[]{:S(2)}) collective-permute-start(bf16[128,3584]{1,0:T(8,128)(2,1)S(1)} %constant_dynamic-update-slice_fusion), channel_id=1, source_target_pairs={{0,16},{16,0},{32,48},{48,32},{64,80},{80,64},{96,112},{112,96},{1... | collective-permute-start | bytes 2752520 | tf_op jit(solution)/shard_map/ppermute | solution.py:19
  82.6 21.6 %collective-permute-start.10 = (f32[256,768]{1,0:T(8,128)S(1)}, f32[256,768]{1,0:T(8,128)S(1)}, u32[]{:S(2)}, u32[]{:S(2)}) collective-permute-start(f32[256,768]{1,0:T(8,128)S(1)} %get-tuple-element.23), channel_id=1, source_target_pairs={{0,1},{1,0},{2,3},{3,2},{4,5},{5,4},{6,7},{7,6},{8,9},{9,8},{10,11... | collective-permute-start | bytes 2359304 | tf_op jit(solution)/shard_map/ppermute | solution.py:23
  84.6 29.0 %collective-permute-start.3 = (bf16[128,3584]{1,0:T(8,128)(2,1)S(1)}, bf16[128,3584]{1,0:T(8,128)(2,1)S(1)}, u32[]{:S(2)}, u32[]{:S(2)}) collective-permute-start(bf16[128,3584]{1,0:T(8,128)(2,1)S(1)} %constant_dynamic-update-slice_fusion), channel_id=1, source_target_pairs={{0,12},{4,8},{8,4},{12,0},{1,13},{5,9},{9,5},{13,1},{2,14},{6,10},... | collective-permute-start | bytes 2752520 | tf_op jit(solution)/shard_map/ppermute | solution.py:19
  99.3 51.7 %copy-start.7 = (bf16[128,3584]{1,0:T(8,128)(2,1)}, bf16[128,3584]{1,0:T(8,128)(2,1)S(1)}, u32[]{:S(2)}) copy-start(bf16[128,3584]{1,0:T(8,128)(2,1)S(1)} %collective-permute-done.2) | copy-start | bytes 2752516
  99.3 51.7 %collective-permute-start.4 = (bf16[128,3584]{1,0:T(8,128)(2,1)S(1)}, bf16[128,3584]{1,0:T(8,128)(2,1)S(1)}, u32[]{:S(2)}, u32[]{:S(2)}) collective-permute-start(bf16[128,3584]{1,0:T(8,128)(2,1)S(1)} %collective-permute-done.2), channel_id=1, source_target_pairs={{0,12},{4,8},{8,4},{12,0},{1,13},{5,9},{9,5},{13,1},{2,14},{6,10},... | collective-permute-start | bytes 2752520 | tf_op jit(solution)/shard_map/ppermute | solution.py:19
  104.6 46.2 %collective-permute-start.11 = (s16[272,768]{1,0:T(8,128)(2,1)S(1)}, s16[272,768]{1,0:T(8,128)(2,1)S(1)}, u32[]{:S(2)}, u32[]{:S(2)}) collective-permute-start(s16[272,768]{1,0:T(8,128)(2,1)S(1)} %pad_add_fusion), channel_id=1, source_target_pairs={{0,2},{2,0},{1,3},{3,1},{4,6},{6,4},{5,7},{7,5},{8,10},{10,8},{9,1... | collective-permute-start | bytes 1253384 | tf_op jit(solution)/shard_map/ppermute | solution.py:23
  151.0 2.0 %copy-start.4 = (bf16[128,3584]{1,0:T(8,128)(2,1)}, bf16[128,3584]{1,0:T(8,128)(2,1)S(1)}, u32[]{:S(2)}) copy-start(bf16[128,3584]{1,0:T(8,128)(2,1)S(1)} %collective-permute-done.4) | copy-start | bytes 2752516
  153.0 4.2 %collective-permute-start.12 = (f32[256,768]{1,0:T(8,128)S(1)}, f32[256,768]{1,0:T(8,128)S(1)}, u32[]{:S(2)}, u32[]{:S(2)}) collective-permute-start(f32[256,768]{1,0:T(8,128)S(1)} %get-tuple-element.13), channel_id=1, source_target_pairs={{0,1},{1,0},{2,3},{3,2},{4,5},{5,4},{6,7},{7,6},{8,9},{9,8},{10,11... | collective-permute-start | bytes 2359304 | tf_op jit(solution)/shard_map/ppermute | solution.py:23
  157.3 4.6 %copy-start = (bf16[768,3584]{1,0:T(8,128)(2,1)S(1)}, bf16[768,3584]{1,0:T(8,128)(2,1)}, u32[]{:S(2)}) copy-start(bf16[768,3584]{1,0:T(8,128)(2,1)} %all-gather.2.cloned.1.call-done) | copy-start | bytes 16515076
  157.3 4.6 %copy-start.3 = (bf16[128,3584]{1,0:T(8,128)(2,1)S(1)}, bf16[128,3584]{1,0:T(8,128)(2,1)}, u32[]{:S(2)}) copy-start(bf16[128,3584]{1,0:T(8,128)(2,1)} %copy-done.2) | copy-start | bytes 2752516
  166.3 3.1 %collective-permute-start.13 = (f32[2,2,16,96]{3,0,1,2:T(2,128)S(1)}, f32[2,2,16,96]{3,0,1,2:T(2,128)S(1)}, u32[]{:S(2)}, u32[]{:S(2)}) collective-permute-start(f32[2,2,16,96]{3,0,1,2:T(2,128)S(1)} %bitcast.52), channel_id=1, source_target_pairs={{0,1},{1,0},{2,3},{3,2},{4,5},{5,4},{6,7},{7,6},{8,9},{9,8},{10,11... | collective-permute-start | bytes 73736 | tf_op jit(solution)/shard_map/ppermute | solution.py:23
  169.4 5.6 %collective-permute-start.14 = (f32[2,16,96]{2,0,1:T(2,128)S(1)}, f32[2,16,96]{2,0,1:T(2,128)S(1)}, u32[]{:S(2)}, u32[]{:S(2)}) collective-permute-start(f32[2,16,96]{2,0,1:T(2,128)S(1)} %fusion.16), channel_id=1, source_target_pairs={{0,4},{4,0},{8,12},{12,8},{1,5},{5,1},{9,13},{13,9},{2,6},{6,2},{1... | collective-permute-start | bytes 36872 | tf_op jit(solution)/shard_map/ppermute | solution.py:19
  175.1 14.3 %collective-permute-start.15 = (f32[2,16,96]{2,1,0:T(8,128)S(1)}, f32[2,16,96]{2,1,0:T(8,128)S(1)}, u32[]{:S(2)}, u32[]{:S(2)}) collective-permute-start(f32[2,16,96]{2,1,0:T(8,128)S(1)} %bitcast.54), channel_id=1, source_target_pairs={{0,2},{2,0},{1,3},{3,1},{4,6},{6,4},{5,7},{7,5},{8,10},{10,8},{9,1... | collective-permute-start | bytes 36872 | tf_op jit(solution)/shard_map/ppermute | solution.py:23
  (2 other events, 2.8 us)
Sparse Core Ops, SparseCore 0:
  9.4 87.5 all-gather.1

commit v3 on v2

--- a/solution.py
+++ b/solution.py
@@ -65,30 +65,24 @@
         second, jnp.concatenate([pair_inputs, token_inputs], axis=0), jnp.concatenate([token_inputs, pair_inputs], axis=0)
     )
     grads = lax.all_gather(token_grads, "y_lo", axis=0, tiled=True)
-    in_near = grow(grow(grow(in_factors, 4), 2), 1)
+    in_got = flip(in_factors, "z_lo", 4)
+    in_near = grow(grow(jnp.concatenate([in_factors, in_got], axis=0), 2), 1)
     in_far = flip(in_near, Y, FACTORS_BY)
     blocks, sent = coded_half(split_sum(rows_of(inputs, in_near), rows_of(inputs, in_far), core))
     right = sum_over_halves(blocks, sent)
 
-    up_near = grow(grow(up_factors, 4), 2)
+    up_near = grow(grow(after(up_factors, in_got), 4), 2)
     next_near = flip(up_near, "z_lo", 1)
     up_far = flip(up_near, Y, FACTORS_BY)
     next_far = flip(next_near, Y, FACTORS_BY)
+    left = lax.optimization_barrier(rows_of(grads, jnp.concatenate([up_near, next_near, up_far, next_far], axis=0)))
     right = right.reshape(-1, 2 * tokens)
-    other = swap(after(right, up_far[:1, :1] + next_far[:1, :1]), "core")
+    half = right.shape[0]
+    head, rest = right[: half // 2], right[half // 2 :]
+    other = swap(head, "core")
+    other = jnp.concatenate([other, swap(after(rest, left[:1, :1] + other[:1, :1]), "core")], axis=0)
     right_near, right_far = jnp.where(core == 0, right, other), jnp.where(core == 0, other, right)
-    half = right.shape[0] // 2
-    left_near, left_far, left_last = lax.optimization_barrier(
-        [rows_of(grads, up) for up in (jnp.concatenate([up_near, next_near], axis=0), up_far, next_far)]
-    )
-    summed = jnp.concatenate(
-        [
-            scores_of(left_near, right_near),
-            scores_of(left_far, right_far[:half]),
-            scores_of(left_last, right_far[half:]),
-        ],
-        axis=0,
-    )
+    summed = jnp.concatenate([scores_of(left[:half], right_near), scores_of(left[half:], right_far)], axis=0)
 
     count = summed.shape[0]
     parts = summed.reshape(count, 2, 2, 2, quarter).transpose(2, 3, 1, 0, 4)

time: 198 us -> 209 us (1.056)
  the two profiles are of different devices: /device:TPU:132 before, /device:TPU:32 now
where the time goes in v3:
time: 209 us; the launch traced here: 208 us
  waiting for transfers between devices  84.9 us (41%)
  starting transfers between devices  83 us (40%)
  between operations  16.3 us (8%)
  matrix products  11.6 us (6%)
  local copies, waits for them, and re-layouts  6.56 us (3%)
  other arithmetic  6.06 us (3%)
    ppermute x11, starting transfers between devices, flip(): lax.ppermute(value, axes, [(i, i ^ bits) for i in range(lax.axis_size(axe...  56.2 us
    ppermute x6, waiting for transfers between devices, swap(): return lax.ppermute(value, axis, SWAP)  45 us
    ppermute x11, waiting for transfers between devices, flip(): lax.ppermute(value, axes, [(i, i ^ bits) for i in range(lax.axis_size(axe...  39.9 us
    ppermute x6, starting transfers between devices, swap(): return lax.ppermute(value, axis, SWAP)  26.7 us
    dot_general x3, matrix products, rows_of(): lax.dot_general(factor_rows, data_rows, (((1,), (1,)), ((), ())), preferr...  10.7 us
  transfers between devices with their start and end apart: 18, of which 10 were waited for; matrix products, arithmetic and copies ran while one was open for 6% of the time, Pallas kernels for 0%

profile of v3, /device:TPU:32, one launch (start us, length us, event | category | flops | bytes accessed | tf_op | source)
XLA Modules:
  0.0 208.4 jit_solution(5793453581683005563)
XLA Ops:
  6.5 9.2 %collective-permute-start = (bf16[32,1024]{1,0:T(8,128)(2,1)}, bf16[32,1024]{1,0:T(8,128)(2,1)S(1)}, u32[]{:S(2)}, u32[]{:S(2)}) collective-permute-start(bf16[32,1024]{1,0:T(8,128)(2,1)} %param.8), channel_id=1, source_target_pairs={{0,64},{16,80},{32,96},{48,112},{64,0},{80,16},{96,32},{112,48},{1... | collective-permute-start | bytes 196616 | tf_op jit(solution)/shard_map/ppermute | solution.py:19
  15.8 5.3 %collective-permute-done = bf16[32,1024]{1,0:T(8,128)(2,1)S(1)} collective-permute-done((bf16[32,1024]{1,0:T(8,128)(2,1)}, bf16[32,1024]{1,0:T(8,128)(2,1)S(1)}, u32[]{:S(2)}, u32[]{:S(2)}) %collective-permute-start) | collective-permute-done | bytes 65568 | tf_op jit(solution)/shard_map/ppermute | solution.py:19
  21.9 4.3 %collective-permute-start.6 = (bf16[64,1024]{1,0:T(8,128)(2,1)S(1)}, bf16[64,1024]{1,0:T(8,128)(2,1)S(1)}, u32[]{:S(2)}, u32[]{:S(2)}) collective-permute-start(bf16[64,1024]{1,0:T(8,128)(2,1)S(1)} %pad_maximum_fusion.3), channel_id=1, source_target_pairs={{0,32},{16,48},{32,0},{48,16},{64,96},{80,112},{96,64},{112,80},{1... | collective-permute-start | bytes 393224 | tf_op jit(solution)/shard_map/ppermute | solution.py:19
  29.8 8.3 %collective-permute-start.1 = (bf16[32,3584]{1,0:T(8,128)(2,1)S(1)}, bf16[32,3584]{1,0:T(8,128)(2,1)S(1)}, u32[]{:S(2)}, u32[]{:S(2)}) collective-permute-start(bf16[32,3584]{1,0:T(8,128)(2,1)S(1)} %get-tuple-element.8), channel_id=1, source_target_pairs={{0,64},{16,80},{32,96},{48,112},{64,0},{80,16},{96,32},{112,48},{1... | collective-permute-start | bytes 688136 | tf_op jit(solution)/shard_map/ppermute | solution.py:19
  38.1 3.5 %collective-permute-start.8 = (bf16[384,1024]{1,0:T(8,128)(2,1)}, bf16[384,1024]{1,0:T(8,128)(2,1)}, u32[]{:S(2)}, u32[]{:S(2)}) collective-permute-start(bf16[384,1024]{1,0:T(8,128)(2,1)} %param.6), channel_id=1, source_target_pairs={{0,4},{4,0},{8,12},{12,8},{1,5},{5,1},{9,13},{13,9},{2,6},{6,2},{1... | collective-permute-start | bytes 2359304 | tf_op jit(solution)/shard_map/ppermute | solution.py:19
  43.6 7.6 %collective-permute-done.1 = bf16[32,3584]{1,0:T(8,128)(2,1)S(1)} collective-permute-done((bf16[32,3584]{1,0:T(8,128)(2,1)S(1)}, bf16[32,3584]{1,0:T(8,128)(2,1)S(1)}, u32[]{:S(2)}, u32[]{:S(2)}) %collective-permute-start.1) | collective-permute-done | bytes 229408 | tf_op jit(solution)/shard_map/ppermute | solution.py:19
  51.2 7.3 %collective-permute-start.2 = (bf16[64,3584]{1,0:T(8,128)(2,1)S(1)}, bf16[64,3584]{1,0:T(8,128)(2,1)S(1)}, u32[]{:S(2)}, u32[]{:S(2)}) collective-permute-start(bf16[64,3584]{1,0:T(8,128)(2,1)S(1)} %pad_maximum_fusion.1), channel_id=1, source_target_pairs={{0,32},{16,48},{32,0},{48,16},{64,96},{80,112},{96,64},{112,80},{1... | collective-permute-start | bytes 1376264 | tf_op jit(solution)/shard_map/ppermute | solution.py:19
  58.6 4.9 %collective-permute-start.9 = (bf16[256,1024]{1,0:T(8,128)(2,1)S(1)}, bf16[256,1024]{1,0:T(8,128)(2,1)S(1)}, u32[]{:S(2)}, u32[]{:S(2)}) collective-permute-start(bf16[256,1024]{1,0:T(8,128)(2,1)S(1)} %constant_dynamic-update-slice_fusion.6), channel_id=1, source_target_pairs={{0,12},{4,8},{8,4},{12,0},{1,13},{5,9},{9,5},{13,1},{2,14},{6,10},... | collective-permute-start | bytes 1572872 | tf_op jit(solution)/shard_map/ppermute | solution.py:19
  63.6 14.7 %collective-permute-done.2 = bf16[64,3584]{1,0:T(8,128)(2,1)S(1)} collective-permute-done((bf16[64,3584]{1,0:T(8,128)(2,1)S(1)}, bf16[64,3584]{1,0:T(8,128)(2,1)S(1)}, u32[]{:S(2)}, u32[]{:S(2)}) %collective-permute-start.2) | collective-permute-done | bytes 458784 | tf_op jit(solution)/shard_map/ppermute | solution.py:19
  78.4 6.1 %collective-permute-start.3 = (bf16[128,3584]{1,0:T(8,128)(2,1)S(1)}, bf16[128,3584]{1,0:T(8,128)(2,1)S(1)}, u32[]{:S(2)}, u32[]{:S(2)}) collective-permute-start(bf16[128,3584]{1,0:T(8,128)(2,1)S(1)} %pad_maximum_fusion), channel_id=1, source_target_pairs={{0,16},{16,0},{32,48},{48,32},{64,80},{80,64},{96,112},{112,96},{1... | collective-permute-start | bytes 2752520 | tf_op jit(solution)/shard_map/ppermute | solution.py:19
  84.5 2.0 fusion.4
  86.5 2.0 broadcast_select_fusion
  91.2 4.4 %collective-permute-start.4 = (bf16[128,3584]{1,0:T(8,128)(2,1)S(1)}, bf16[128,3584]{1,0:T(8,128)(2,1)S(1)}, u32[]{:S(2)}, u32[]{:S(2)}) collective-permute-start(bf16[128,3584]{1,0:T(8,128)(2,1)S(1)} %pad_maximum_fusion), channel_id=1, source_target_pairs={{0,12},{4,8},{8,4},{12,0},{1,13},{5,9},{9,5},{13,1},{2,14},{6,10},... | collective-permute-start | bytes 2752520 | tf_op jit(solution)/shard_map/ppermute | solution.py:19
  96.3 8.5 %collective-permute-done.3 = bf16[128,3584]{1,0:T(8,128)(2,1)S(1)} collective-permute-done((bf16[128,3584]{1,0:T(8,128)(2,1)S(1)}, bf16[128,3584]{1,0:T(8,128)(2,1)S(1)}, u32[]{:S(2)}, u32[]{:S(2)}) %collective-permute-start.3) | collective-permute-done | bytes 917536 | tf_op jit(solution)/shard_map/ppermute | solution.py:19
  104.8 4.4 %collective-permute-start.5 = (bf16[128,3584]{1,0:T(8,128)(2,1)S(1)}, bf16[128,3584]{1,0:T(8,128)(2,1)S(1)}, u32[]{:S(2)}, u32[]{:S(2)}) collective-permute-start(bf16[128,3584]{1,0:T(8,128)(2,1)S(1)} %collective-permute-done.3), channel_id=1, source_target_pairs={{0,12},{4,8},{8,4},{12,0},{1,13},{5,9},{9,5},{13,1},{2,14},{6,10},... | collective-permute-start | bytes 2752520 | tf_op jit(solution)/shard_map/ppermute | solution.py:19
  109.6 9.6 %collective-permute-start.11 = (s16[272,768]{1,0:T(8,128)(2,1)S(1)}, s16[272,768]{1,0:T(8,128)(2,1)S(1)}, u32[]{:S(2)}, u32[]{:S(2)}) collective-permute-start(s16[272,768]{1,0:T(8,128)(2,1)S(1)} %pad_add_fusion), channel_id=1, source_target_pairs={{0,2},{2,0},{1,3},{3,1},{4,6},{6,4},{5,7},{7,5},{8,10},{10,8},{9,1... | collective-permute-start | bytes 1253384 | tf_op jit(solution)/shard_map/ppermute | solution.py:23
  120.2 37.5 %collective-permute-done.11 = s16[272,768]{1,0:T(8,128)(2,1)S(1)} collective-permute-done((s16[272,768]{1,0:T(8,128)(2,1)S(1)}, s16[272,768]{1,0:T(8,128)(2,1)S(1)}, u32[]{:S(2)}, u32[]{:S(2)}) %collective-permute-start.11) | collective-permute-done | bytes 417824 | tf_op jit(solution)/shard_map/ppermute | solution.py:23
  158.0 1.9 collective-permute-start.12
  163.2 6.7 %fusion.45 = f32[512,768]{1,0:T(8,128)S(1)} fusion(bf16[512,3584]{1,0:T(8,128)(2,1)} %constant_dynamic-update-slice_fusion, bf16[768,3584]{1,0:T(8,128)(2,1)} %all-gather.2.cloned.1.call-done), kind=kOutput, calls=%fused_computation.122 | convolution fusion | flops 2818572288 | bytes 10747904 | tf_op jit(solution)/shard_map/dot_general | solution.py:15
  171.8 2.0 collective-permute-start.13
  177.5 2.0 collective-permute-start.14
  182.6 3.7 %collective-permute-done.15 = f32[2,16,96]{2,0,1:T(2,128)S(1)} collective-permute-done((f32[2,16,96]{2,0,1:T(2,128)S(1)}, f32[2,16,96]{2,0,1:T(2,128)S(1)}, u32[]{:S(2)}, u32[]{:S(2)}) %collective-permute-start.15) | collective-permute-done | bytes 12320 | tf_op jit(solution)/shard_map/ppermute | solution.py:19
  186.3 9.3 %collective-permute-start.16 = (f32[2,16,96]{2,1,0:T(8,128)S(1)}, f32[2,16,96]{2,1,0:T(8,128)S(1)}, u32[]{:S(2)}, u32[]{:S(2)}) collective-permute-start(f32[2,16,96]{2,1,0:T(8,128)S(1)} %bitcast.62), channel_id=1, source_target_pairs={{0,2},{2,0},{1,3},{3,1},{4,6},{6,4},{5,7},{7,5},{8,10},{10,8},{9,1... | collective-permute-start | bytes 36872 | tf_op jit(solution)/shard_map/ppermute | solution.py:23
  195.6 5.0 %collective-permute-done.16 = f32[2,16,96]{2,1,0:T(8,128)S(1)} collective-permute-done((f32[2,16,96]{2,1,0:T(8,128)S(1)}, f32[2,16,96]{2,1,0:T(8,128)S(1)}, u32[]{:S(2)}, u32[]{:S(2)}) %collective-permute-start.16) | collective-permute-done | bytes 12320 | tf_op jit(solution)/shard_map/ppermute | solution.py:23
  (63 shorter events, 21.8 us)
Async XLA Ops:
  6.5 35.1 %copy-start.1 = (bf16[32,1024]{1,0:T(8,128)(2,1)S(1)}, bf16[32,1024]{1,0:T(8,128)(2,1)}, u32[]{:S(2)}) copy-start(bf16[32,1024]{1,0:T(8,128)(2,1)} %param.8) | copy-start | bytes 196612
  6.5 156.7 %all-gather.2.cloned.1.call-start = ((), (), s32[]{:S(2)}) async-start(), calls=%async_computation | async-start | bytes 8257536 | tf_op jit(solution)/shard_map/all_gather | solution.py:67
  6.5 14.6 %collective-permute-start = (bf16[32,1024]{1,0:T(8,128)(2,1)}, bf16[32,1024]{1,0:T(8,128)(2,1)S(1)}, u32[]{:S(2)}, u32[]{:S(2)}) collective-permute-start(bf16[32,1024]{1,0:T(8,128)(2,1)} %param.8), channel_id=1, source_target_pairs={{0,64},{16,80},{32,96},{48,112},{64,0},{80,16},{96,32},{112,48},{1... | collective-permute-start | bytes 196616 | tf_op jit(solution)/shard_map/ppermute | solution.py:19
  21.9 19.7 %collective-permute-start.6 = (bf16[64,1024]{1,0:T(8,128)(2,1)S(1)}, bf16[64,1024]{1,0:T(8,128)(2,1)S(1)}, u32[]{:S(2)}, u32[]{:S(2)}) collective-permute-start(bf16[64,1024]{1,0:T(8,128)(2,1)S(1)} %pad_maximum_fusion.3), channel_id=1, source_target_pairs={{0,32},{16,48},{32,0},{48,16},{64,96},{80,112},{96,64},{112,80},{1... | collective-permute-start | bytes 393224 | tf_op jit(solution)/shard_map/ppermute | solution.py:19
  29.8 54.7 %copy-start.2 = (bf16[384,1024]{1,0:T(8,128)(2,1)S(1)}, bf16[384,1024]{1,0:T(8,128)(2,1)}, u32[]{:S(2)}) copy-start(bf16[384,1024]{1,0:T(8,128)(2,1)} %param.6) | copy-start | bytes 2359300
  29.8 21.4 %collective-permute-start.1 = (bf16[32,3584]{1,0:T(8,128)(2,1)S(1)}, bf16[32,3584]{1,0:T(8,128)(2,1)S(1)}, u32[]{:S(2)}, u32[]{:S(2)}) collective-permute-start(bf16[32,3584]{1,0:T(8,128)(2,1)S(1)} %get-tuple-element.8), channel_id=1, source_target_pairs={{0,64},{16,80},{32,96},{48,112},{64,0},{80,16},{96,32},{112,48},{1... | collective-permute-start | bytes 688136 | tf_op jit(solution)/shard_map/ppermute | solution.py:19
  38.1 46.4 %collective-permute-start.8 = (bf16[384,1024]{1,0:T(8,128)(2,1)}, bf16[384,1024]{1,0:T(8,128)(2,1)}, u32[]{:S(2)}, u32[]{:S(2)}) collective-permute-start(bf16[384,1024]{1,0:T(8,128)(2,1)} %param.6), channel_id=1, source_target_pairs={{0,4},{4,0},{8,12},{12,8},{1,5},{5,1},{9,13},{13,9},{2,6},{6,2},{1... | collective-permute-start | bytes 2359304 | tf_op jit(solution)/shard_map/ppermute | solution.py:19
  41.7 16.9 %collective-permute-start.7 = (bf16[128,1024]{1,0:T(8,128)(2,1)S(1)}, bf16[128,1024]{1,0:T(8,128)(2,1)S(1)}, u32[]{:S(2)}, u32[]{:S(2)}) collective-permute-start(bf16[128,1024]{1,0:T(8,128)(2,1)S(1)} %pad_maximum_fusion.2), channel_id=1, source_target_pairs={{0,16},{16,0},{32,48},{48,32},{64,80},{80,64},{96,112},{112,96},{1... | collective-permute-start | bytes 786440 | tf_op jit(solution)/shard_map/ppermute | solution.py:19
  51.2 27.1 %collective-permute-start.2 = (bf16[64,3584]{1,0:T(8,128)(2,1)S(1)}, bf16[64,3584]{1,0:T(8,128)(2,1)S(1)}, u32[]{:S(2)}, u32[]{:S(2)}) collective-permute-start(bf16[64,3584]{1,0:T(8,128)(2,1)S(1)} %pad_maximum_fusion.1), channel_id=1, source_target_pairs={{0,32},{16,48},{32,0},{48,16},{64,96},{80,112},{96,64},{112,80},{1... | collective-permute-start | bytes 1376264 | tf_op jit(solution)/shard_map/ppermute | solution.py:19
  58.6 27.9 %collective-permute-start.9 = (bf16[256,1024]{1,0:T(8,128)(2,1)S(1)}, bf16[256,1024]{1,0:T(8,128)(2,1)S(1)}, u32[]{:S(2)}, u32[]{:S(2)}) collective-permute-start(bf16[256,1024]{1,0:T(8,128)(2,1)S(1)} %constant_dynamic-update-slice_fusion.6), channel_id=1, source_target_pairs={{0,12},{4,8},{8,4},{12,0},{1,13},{5,9},{9,5},{13,1},{2,14},{6,10},... | collective-permute-start | bytes 1572872 | tf_op jit(solution)/shard_map/ppermute | solution.py:19
  78.4 26.5 %collective-permute-start.3 = (bf16[128,3584]{1,0:T(8,128)(2,1)S(1)}, bf16[128,3584]{1,0:T(8,128)(2,1)S(1)}, u32[]{:S(2)}, u32[]{:S(2)}) collective-permute-start(bf16[128,3584]{1,0:T(8,128)(2,1)S(1)} %pad_maximum_fusion), channel_id=1, source_target_pairs={{0,16},{16,0},{32,48},{48,32},{64,80},{80,64},{96,112},{112,96},{1... | collective-permute-start | bytes 2752520 | tf_op jit(solution)/shard_map/ppermute | solution.py:19
  88.5 20.7 %collective-permute-start.10 = (f32[256,768]{1,0:T(8,128)S(1)}, f32[256,768]{1,0:T(8,128)S(1)}, u32[]{:S(2)}, u32[]{:S(2)}) collective-permute-start(f32[256,768]{1,0:T(8,128)S(1)} %get-tuple-element.17), channel_id=1, source_target_pairs={{0,1},{1,0},{2,3},{3,2},{4,5},{5,4},{6,7},{7,6},{8,9},{9,8},{10,11... | collective-permute-start | bytes 2359304 | tf_op jit(solution)/shard_map/ppermute | solution.py:23
  91.2 68.8 %collective-permute-start.4 = (bf16[128,3584]{1,0:T(8,128)(2,1)S(1)}, bf16[128,3584]{1,0:T(8,128)(2,1)S(1)}, u32[]{:S(2)}, u32[]{:S(2)}) collective-permute-start(bf16[128,3584]{1,0:T(8,128)(2,1)S(1)} %pad_maximum_fusion), channel_id=1, source_target_pairs={{0,12},{4,8},{8,4},{12,0},{1,13},{5,9},{9,5},{13,1},{2,14},{6,10},... | collective-permute-start | bytes 2752520 | tf_op jit(solution)/shard_map/ppermute | solution.py:19
  104.8 57.3 %collective-permute-start.5 = (bf16[128,3584]{1,0:T(8,128)(2,1)S(1)}, bf16[128,3584]{1,0:T(8,128)(2,1)S(1)}, u32[]{:S(2)}, u32[]{:S(2)}) collective-permute-start(bf16[128,3584]{1,0:T(8,128)(2,1)S(1)} %collective-permute-done.3), channel_id=1, source_target_pairs={{0,12},{4,8},{8,4},{12,0},{1,13},{5,9},{9,5},{13,1},{2,14},{6,10},... | collective-permute-start | bytes 2752520 | tf_op jit(solution)/shard_map/ppermute | solution.py:19
  109.6 48.1 %collective-permute-start.11 = (s16[272,768]{1,0:T(8,128)(2,1)S(1)}, s16[272,768]{1,0:T(8,128)(2,1)S(1)}, u32[]{:S(2)}, u32[]{:S(2)}) collective-permute-start(s16[272,768]{1,0:T(8,128)(2,1)S(1)} %pad_add_fusion), channel_id=1, source_target_pairs={{0,2},{2,0},{1,3},{3,1},{4,6},{6,4},{5,7},{7,5},{8,10},{10,8},{9,1... | collective-permute-start | bytes 1253384 | tf_op jit(solution)/shard_map/ppermute | solution.py:23
  158.0 3.6 %collective-permute-start.12 = (f32[128,768]{1,0:T(8,128)S(1)}, f32[128,768]{1,0:T(8,128)S(1)}, u32[]{:S(2)}, u32[]{:S(2)}) collective-permute-start(f32[128,768]{1,0:T(8,128)S(1)} %bitcast.56), channel_id=1, source_target_pairs={{0,1},{1,0},{2,3},{3,2},{4,5},{5,4},{6,7},{7,6},{8,9},{9,8},{10,11... | collective-permute-start | bytes 1179656 | tf_op jit(solution)/shard_map/ppermute | solution.py:23
  170.0 1.8 copy-start
  171.8 3.6 %collective-permute-start.13 = (f32[128,768]{1,0:T(8,128)S(1)}, f32[128,768]{1,0:T(8,128)S(1)}, u32[]{:S(2)}, u32[]{:S(2)}) collective-permute-start(f32[128,768]{1,0:T(8,128)S(1)} %bitcast.57), channel_id=1, source_target_pairs={{0,1},{1,0},{2,3},{3,2},{4,5},{5,4},{6,7},{7,6},{8,9},{9,8},{10,11... | collective-permute-start | bytes 1179656 | tf_op jit(solution)/shard_map/ppermute | solution.py:23
  177.5 3.1 %collective-permute-start.14 = (f32[2,2,16,96]{3,0,1,2:T(2,128)S(1)}, f32[2,2,16,96]{3,0,1,2:T(2,128)S(1)}, u32[]{:S(2)}, u32[]{:S(2)}) collective-permute-start(f32[2,2,16,96]{3,0,1,2:T(2,128)S(1)} %bitcast.60), channel_id=1, source_target_pairs={{0,1},{1,0},{2,3},{3,2},{4,5},{5,4},{6,7},{7,6},{8,9},{9,8},{10,11... | collective-permute-start | bytes 73736 | tf_op jit(solution)/shard_map/ppermute | solution.py:23
  180.6 5.6 %collective-permute-start.15 = (f32[2,16,96]{2,0,1:T(2,128)S(1)}, f32[2,16,96]{2,0,1:T(2,128)S(1)}, u32[]{:S(2)}, u32[]{:S(2)}) collective-permute-start(f32[2,16,96]{2,0,1:T(2,128)S(1)} %fusion.8), channel_id=1, source_target_pairs={{0,4},{4,0},{8,12},{12,8},{1,5},{5,1},{9,13},{13,9},{2,6},{6,2},{1... | collective-permute-start | bytes 36872 | tf_op jit(solution)/shard_map/ppermute | solution.py:19
  186.3 14.3 %collective-permute-start.16 = (f32[2,16,96]{2,1,0:T(8,128)S(1)}, f32[2,16,96]{2,1,0:T(8,128)S(1)}, u32[]{:S(2)}, u32[]{:S(2)}) collective-permute-start(f32[2,16,96]{2,1,0:T(8,128)S(1)} %bitcast.62), channel_id=1, source_target_pairs={{0,2},{2,0},{1,3},{3,1},{4,6},{6,4},{5,7},{7,5},{8,10},{10,8},{9,1... | collective-permute-start | bytes 36872 | tf_op jit(solution)/shard_map/ppermute | solution.py:23
Sparse Core Ops, SparseCore 0:
  41.8 79.8 all-gather.1

commit v4 on v2

--- a/solution.py
+++ b/solution.py
@@ -74,13 +74,12 @@
     next_near = flip(up_near, "z_lo", 1)
     up_far = flip(up_near, Y, FACTORS_BY)
     next_far = flip(next_near, Y, FACTORS_BY)
-    right = right.reshape(-1, 2 * tokens)
-    other = swap(after(right, up_far[:1, :1] + next_far[:1, :1]), "core")
+    ups = (jnp.concatenate([up_near, next_near], axis=0), up_far, next_far)
+    left_near, left_far, left_last = lax.optimization_barrier([rows_of(grads, up) for up in ups])
+    right = after(right.reshape(-1, 2 * tokens), left_near[:1, :1] + left_far[:1, :1] + left_last[:1, :1])
+    other = swap(right, "core")
     right_near, right_far = jnp.where(core == 0, right, other), jnp.where(core == 0, other, right)
     half = right.shape[0] // 2
-    left_near, left_far, left_last = lax.optimization_barrier(
-        [rows_of(grads, up) for up in (jnp.concatenate([up_near, next_near], axis=0), up_far, next_far)]
-    )
     summed = jnp.concatenate(
         [
             scores_of(left_near, right_near),

time: 198 us -> 210 us (1.061)
  the two profiles are of different devices: /device:TPU:132 before, /device:TPU:2 now
where the time goes in v4:
time: 210 us; the launch traced here: 209 us
  waiting for transfers between devices  103 us (49%)
  starting transfers between devices  67.4 us (32%)
  matrix products  15.9 us (8%)
  between operations  15.7 us (7%)
  local copies, waits for them, and re-layouts  4.09 us (2%)
  other arithmetic  2.86 us (1%)
    ppermute x11, waiting for transfers between devices, flip(): lax.ppermute(value, axes, [(i, i ^ bits) for i in range(lax.axis_size(axe...  73.8 us
    ppermute x11, starting transfers between devices, flip(): lax.ppermute(value, axes, [(i, i ^ bits) for i in range(lax.axis_size(axe...  43.7 us
    ppermute x5, waiting for transfers between devices, swap(): return lax.ppermute(value, axis, SWAP)  28.8 us
    ppermute x5, starting transfers between devices, swap(): return lax.ppermute(value, axis, SWAP)  23.7 us
    dot_general x5, matrix products, rows_of(): lax.dot_general(factor_rows, data_rows, (((1,), (1,)), ((), ())), preferr...  15 us
  transfers between devices with their start and end apart: 17, of which 11 were waited for; matrix products, arithmetic and copies ran while one was open for 8% of the time, Pallas kernels for 0%

profile of v4, /device:TPU:2, one launch (start us, length us, event | category | flops | bytes accessed | tf_op | source)
XLA Modules:
  0.0 209.2 jit_solution(18445678759631739261)
XLA Ops:
  7.3 9.1 %collective-permute-start.5 = (bf16[32,1024]{1,0:T(8,128)(2,1)}, bf16[32,1024]{1,0:T(8,128)(2,1)S(1)}, u32[]{:S(2)}, u32[]{:S(2)}) collective-permute-start(bf16[32,1024]{1,0:T(8,128)(2,1)} %param.8), channel_id=1, source_target_pairs={{0,64},{16,80},{32,96},{48,112},{64,0},{80,16},{96,32},{112,48},{1... | collective-permute-start | bytes 196616 | tf_op jit(solution)/shard_map/ppermute | solution.py:19
  18.3 3.5 %collective-permute-start.8 = (bf16[384,1024]{1,0:T(8,128)(2,1)}, bf16[384,1024]{1,0:T(8,128)(2,1)}, u32[]{:S(2)}, u32[]{:S(2)}) collective-permute-start(bf16[384,1024]{1,0:T(8,128)(2,1)} %param.6), channel_id=1, source_target_pairs={{0,4},{4,0},{8,12},{12,8},{1,5},{5,1},{9,13},{13,9},{2,6},{6,2},{1... | collective-permute-start | bytes 2359304 | tf_op jit(solution)/shard_map/ppermute | solution.py:19
  23.9 12.1 %collective-permute-start.6 = (bf16[64,1024]{1,0:T(8,128)(2,1)S(1)}, bf16[64,1024]{1,0:T(8,128)(2,1)S(1)}, u32[]{:S(2)}, u32[]{:S(2)}) collective-permute-start(bf16[64,1024]{1,0:T(8,128)(2,1)S(1)} %pad_maximum_fusion.2), channel_id=1, source_target_pairs={{0,32},{16,48},{32,0},{48,16},{64,96},{80,112},{96,64},{112,80},{1... | collective-permute-start | bytes 393224 | tf_op jit(solution)/shard_map/ppermute | solution.py:19
  36.6 12.6 %collective-permute-done.6 = bf16[64,1024]{1,0:T(8,128)(2,1)S(1)} collective-permute-done((bf16[64,1024]{1,0:T(8,128)(2,1)S(1)}, bf16[64,1024]{1,0:T(8,128)(2,1)S(1)}, u32[]{:S(2)}, u32[]{:S(2)}) %collective-permute-start.6) | collective-permute-done | bytes 131104 | tf_op jit(solution)/shard_map/ppermute | solution.py:19
  51.3 7.6 %collective-permute-done.7 = bf16[128,1024]{1,0:T(8,128)(2,1)S(1)} collective-permute-done((bf16[128,1024]{1,0:T(8,128)(2,1)S(1)}, bf16[128,1024]{1,0:T(8,128)(2,1)S(1)}, u32[]{:S(2)}, u32[]{:S(2)}) %collective-permute-start.7) | collective-permute-done | bytes 262176 | tf_op jit(solution)/shard_map/ppermute | solution.py:19
  58.9 4.9 %collective-permute-start.9 = (bf16[256,1024]{1,0:T(8,128)(2,1)S(1)}, bf16[256,1024]{1,0:T(8,128)(2,1)S(1)}, u32[]{:S(2)}, u32[]{:S(2)}) collective-permute-start(bf16[256,1024]{1,0:T(8,128)(2,1)S(1)} %constant_dynamic-update-slice_fusion.3), channel_id=1, source_target_pairs={{0,12},{4,8},{8,4},{12,0},{1,13},{5,9},{9,5},{13,1},{2,14},{6,10},... | collective-permute-start | bytes 1572872 | tf_op jit(solution)/shard_map/ppermute | solution.py:19
  67.9 6.8 %collective-permute-done.9 = bf16[256,1024]{1,0:T(8,128)(2,1)S(1)} collective-permute-done((bf16[256,1024]{1,0:T(8,128)(2,1)S(1)}, bf16[256,1024]{1,0:T(8,128)(2,1)S(1)}, u32[]{:S(2)}, u32[]{:S(2)}) %collective-permute-start.9) | collective-permute-done | bytes 524320 | tf_op jit(solution)/shard_map/ppermute | solution.py:19
  74.7 2.0 broadcast_select_fusion.1
  79.3 8.1 %collective-permute-done.1 = bf16[64,3584]{1,0:T(8,128)(2,1)S(1)} collective-permute-done((bf16[64,3584]{1,0:T(8,128)(2,1)S(1)}, bf16[64,3584]{1,0:T(8,128)(2,1)S(1)}, u32[]{:S(2)}, u32[]{:S(2)}) %collective-permute-start.1) | collective-permute-done | bytes 458784 | tf_op jit(solution)/shard_map/ppermute | solution.py:19
  90.2 2.2 %collective-permute-start.3 = (bf16[128,3584]{1,0:T(8,128)(2,1)}, bf16[128,3584]{1,0:T(8,128)(2,1)}, u32[]{:S(2)}, u32[]{:S(2)}) collective-permute-start(bf16[128,3584]{1,0:T(8,128)(2,1)} %constant_dynamic-update-slice_fusion), channel_id=1, source_target_pairs={{0,12},{4,8},{8,4},{12,0},{1,13},{5,9},{9,5},{13,1},{2,14},{6,10},... | collective-permute-start | bytes 2752520 | tf_op jit(solution)/shard_map/ppermute | solution.py:19
  92.8 13.8 %collective-permute-start.11 = (s16[272,768]{1,0:T(8,128)(2,1)S(1)}, s16[272,768]{1,0:T(8,128)(2,1)S(1)}, u32[]{:S(2)}, u32[]{:S(2)}) collective-permute-start(s16[272,768]{1,0:T(8,128)(2,1)S(1)} %pad_add_fusion), channel_id=1, source_target_pairs={{0,2},{2,0},{1,3},{3,1},{4,6},{6,4},{5,7},{7,5},{8,10},{10,8},{9,1... | collective-permute-start | bytes 1253384 | tf_op jit(solution)/shard_map/ppermute | solution.py:23
  106.6 33.9 %collective-permute-done.2 = bf16[128,3584]{1,0:T(8,128)(2,1)} collective-permute-done((bf16[128,3584]{1,0:T(8,128)(2,1)}, bf16[128,3584]{1,0:T(8,128)(2,1)}, u32[]{:S(2)}, u32[]{:S(2)}) %collective-permute-start.2) | collective-permute-done | bytes 917536 | tf_op jit(solution)/shard_map/ppermute | solution.py:19
  140.5 2.2 %collective-permute-start.4 = (bf16[128,3584]{1,0:T(8,128)(2,1)}, bf16[128,3584]{1,0:T(8,128)(2,1)}, u32[]{:S(2)}, u32[]{:S(2)}) collective-permute-start(bf16[128,3584]{1,0:T(8,128)(2,1)} %collective-permute-done.2), channel_id=1, source_target_pairs={{0,12},{4,8},{8,4},{12,0},{1,13},{5,9},{9,5},{13,1},{2,14},{6,10},... | collective-permute-start | bytes 2752520 | tf_op jit(solution)/shard_map/ppermute | solution.py:19
  142.7 15.8 %collective-permute-done.11 = s16[272,768]{1,0:T(8,128)(2,1)S(1)} collective-permute-done((s16[272,768]{1,0:T(8,128)(2,1)S(1)}, s16[272,768]{1,0:T(8,128)(2,1)S(1)}, u32[]{:S(2)}, u32[]{:S(2)}) %collective-permute-start.11) | collective-permute-done | bytes 417824 | tf_op jit(solution)/shard_map/ppermute | solution.py:23
  158.7 4.8 %fusion.55 = f32[128,768]{1,0:T(8,128)S(1)} fusion(bf16[128,3584]{1,0:T(8,128)(2,1)} %collective-permute-done.3, bf16[768,3584]{1,0:T(8,128)(2,1)} %all-gather.2.cloned.1.call-done), kind=kOutput, calls=%fused_computation.126 | convolution fusion | flops 704643072 | bytes 6815744 | tf_op jit(solution)/shard_map/dot_general | solution.py:15
  163.6 2.8 %fusion = f32[256,768]{1,0:T(8,128)S(1)} fusion(bf16[768,3584]{1,0:T(8,128)(2,1)S(1)} %copy-done, bf16[128,3584]{1,0:T(8,128)(2,1)} %collective-permute-done.2, bf16[64,3584]{1,0:T(8,128)(2,1)S(1)} %collective-permute-done.1, bf16[32,3584]{1,0:T(8,128)(2,1)S(1)} %collective-permute-done, bf16[32,3584]{1,0:T(8,128)(2,1)S(1)} %copy-done.1), kind=kOutput, calls=%fused_computation | convolution fusion | flops 1416626176 | bytes 8126464 | tf_op jit(solution)/shard_map/dot_general | solution.py:15
  166.4 3.3 %fusion.56 = f32[128,768]{1,0:T(8,128)S(1)} fusion(bf16[128,3584]{1,0:T(8,128)(2,1)} %collective-permute-done.4, bf16[768,3584]{1,0:T(8,128)(2,1)S(1)} %copy-done), kind=kOutput, calls=%fused_computation.127 | convolution fusion | flops 704643072 | bytes 6815744 | tf_op jit(solution)/shard_map/dot_general | solution.py:15
  173.3 2.1 collective-permute-start.12
  175.4 2.2 %collective-permute-done.12 = f32[256,768]{1,0:T(8,128)S(1)} collective-permute-done((f32[256,768]{1,0:T(8,128)S(1)}, f32[256,768]{1,0:T(8,128)S(1)}, u32[]{:S(2)}, u32[]{:S(2)}) %collective-permute-start.12) | collective-permute-done | bytes 786464 | tf_op jit(solution)/shard_map/ppermute | solution.py:23
  178.3 2.0 collective-permute-start.13
  181.4 2.0 collective-permute-start.14
  183.5 3.6 %collective-permute-done.14 = f32[2,16,96]{2,0,1:T(2,128)S(1)} collective-permute-done((f32[2,16,96]{2,0,1:T(2,128)S(1)}, f32[2,16,96]{2,0,1:T(2,128)S(1)}, u32[]{:S(2)}, u32[]{:S(2)}) %collective-permute-start.14) | collective-permute-done | bytes 12320 | tf_op jit(solution)/shard_map/ppermute | solution.py:19
  187.1 3.9 %collective-permute-start.15 = (f32[2,16,96]{2,1,0:T(8,128)S(1)}, f32[2,16,96]{2,1,0:T(8,128)S(1)}, u32[]{:S(2)}, u32[]{:S(2)}) collective-permute-start(f32[2,16,96]{2,1,0:T(8,128)S(1)} %bitcast.53), channel_id=1, source_target_pairs={{0,2},{2,0},{1,3},{3,1},{4,6},{6,4},{5,7},{7,5},{8,10},{10,8},{9,1... | collective-permute-start | bytes 36872 | tf_op jit(solution)/shard_map/ppermute | solution.py:23
  191.0 10.4 %collective-permute-done.15 = f32[2,16,96]{2,1,0:T(8,128)S(1)} collective-permute-done((f32[2,16,96]{2,1,0:T(8,128)S(1)}, f32[2,16,96]{2,1,0:T(8,128)S(1)}, u32[]{:S(2)}, u32[]{:S(2)}) %collective-permute-start.15) | collective-permute-done | bytes 12320 | tf_op jit(solution)/shard_map/ppermute | solution.py:23
  (62 shorter events, 21.7 us)
Async XLA Ops:
  6.5 42.7 %copy-start.4 = (bf16[32,1024]{1,0:T(8,128)(2,1)S(1)}, bf16[32,1024]{1,0:T(8,128)(2,1)}, u32[]{:S(2)}) copy-start(bf16[32,1024]{1,0:T(8,128)(2,1)} %param.8) | copy-start | bytes 196612
  6.5 29.4 %copy-start.1 = (bf16[32,3584]{1,0:T(8,128)(2,1)S(1)}, bf16[32,3584]{1,0:T(8,128)(2,1)}, u32[]{:S(2)}) copy-start(bf16[32,3584]{1,0:T(8,128)(2,1)} %param.7) | copy-start | bytes 688132
  6.5 59.3 %copy-start.5 = (bf16[384,1024]{1,0:T(8,128)(2,1)S(1)}, bf16[384,1024]{1,0:T(8,128)(2,1)}, u32[]{:S(2)}) copy-start(bf16[384,1024]{1,0:T(8,128)(2,1)} %param.6) | copy-start | bytes 2359300
  6.5 152.2 %all-gather.2.cloned.1.call-start = ((), (), s32[]{:S(2)}) async-start(), calls=%async_computation | async-start | bytes 8257536 | tf_op jit(solution)/shard_map/all_gather | solution.py:67
  7.3 15.8 %collective-permute-start.5 = (bf16[32,1024]{1,0:T(8,128)(2,1)}, bf16[32,1024]{1,0:T(8,128)(2,1)S(1)}, u32[]{:S(2)}, u32[]{:S(2)}) collective-permute-start(bf16[32,1024]{1,0:T(8,128)(2,1)} %param.8), channel_id=1, source_target_pairs={{0,64},{16,80},{32,96},{48,112},{64,0},{80,16},{96,32},{112,48},{1... | collective-permute-start | bytes 196616 | tf_op jit(solution)/shard_map/ppermute | solution.py:19
  16.4 47.5 %collective-permute-start = (bf16[32,3584]{1,0:T(8,128)(2,1)}, bf16[32,3584]{1,0:T(8,128)(2,1)S(1)}, u32[]{:S(2)}, u32[]{:S(2)}) collective-permute-start(bf16[32,3584]{1,0:T(8,128)(2,1)} %param.7), channel_id=1, source_target_pairs={{0,64},{16,80},{32,96},{48,112},{64,0},{80,16},{96,32},{112,48},{1... | collective-permute-start | bytes 688136 | tf_op jit(solution)/shard_map/ppermute | solution.py:19
  18.3 47.6 %collective-permute-start.8 = (bf16[384,1024]{1,0:T(8,128)(2,1)}, bf16[384,1024]{1,0:T(8,128)(2,1)}, u32[]{:S(2)}, u32[]{:S(2)}) collective-permute-start(bf16[384,1024]{1,0:T(8,128)(2,1)} %param.6), channel_id=1, source_target_pairs={{0,4},{4,0},{8,12},{12,8},{1,5},{5,1},{9,13},{13,9},{2,6},{6,2},{1... | collective-permute-start | bytes 2359304 | tf_op jit(solution)/shard_map/ppermute | solution.py:19
  23.9 25.4 %collective-permute-start.6 = (bf16[64,1024]{1,0:T(8,128)(2,1)S(1)}, bf16[64,1024]{1,0:T(8,128)(2,1)S(1)}, u32[]{:S(2)}, u32[]{:S(2)}) collective-permute-start(bf16[64,1024]{1,0:T(8,128)(2,1)S(1)} %pad_maximum_fusion.2), channel_id=1, source_target_pairs={{0,32},{16,48},{32,0},{48,16},{64,96},{80,112},{96,64},{112,80},{1... | collective-permute-start | bytes 393224 | tf_op jit(solution)/shard_map/ppermute | solution.py:19
  49.3 9.6 %collective-permute-start.7 = (bf16[128,1024]{1,0:T(8,128)(2,1)S(1)}, bf16[128,1024]{1,0:T(8,128)(2,1)S(1)}, u32[]{:S(2)}, u32[]{:S(2)}) collective-permute-start(bf16[128,1024]{1,0:T(8,128)(2,1)S(1)} %pad_maximum_fusion.1), channel_id=1, source_target_pairs={{0,16},{16,0},{32,48},{48,32},{64,80},{80,64},{96,112},{112,96},{1... | collective-permute-start | bytes 786440 | tf_op jit(solution)/shard_map/ppermute | solution.py:19
  58.9 15.7 %collective-permute-start.9 = (bf16[256,1024]{1,0:T(8,128)(2,1)S(1)}, bf16[256,1024]{1,0:T(8,128)(2,1)S(1)}, u32[]{:S(2)}, u32[]{:S(2)}) collective-permute-start(bf16[256,1024]{1,0:T(8,128)(2,1)S(1)} %constant_dynamic-update-slice_fusion.3), channel_id=1, source_target_pairs={{0,12},{4,8},{8,4},{12,0},{1,13},{5,9},{9,5},{13,1},{2,14},{6,10},... | collective-permute-start | bytes 1572872 | tf_op jit(solution)/shard_map/ppermute | solution.py:19
  63.9 23.5 %collective-permute-start.1 = (bf16[64,3584]{1,0:T(8,128)(2,1)S(1)}, bf16[64,3584]{1,0:T(8,128)(2,1)S(1)}, u32[]{:S(2)}, u32[]{:S(2)}) collective-permute-start(bf16[64,3584]{1,0:T(8,128)(2,1)S(1)} %pad_maximum_fusion), channel_id=1, source_target_pairs={{0,32},{16,48},{32,0},{48,16},{64,96},{80,112},{96,64},{112,80},{1... | collective-permute-start | bytes 1376264 | tf_op jit(solution)/shard_map/ppermute | solution.py:19
  76.7 15.7 %collective-permute-start.10 = (f32[256,768]{1,0:T(8,128)S(1)}, f32[256,768]{1,0:T(8,128)S(1)}, u32[]{:S(2)}, u32[]{:S(2)}) collective-permute-start(f32[256,768]{1,0:T(8,128)S(1)} %get-tuple-element.21), channel_id=1, source_target_pairs={{0,1},{1,0},{2,3},{3,2},{4,5},{5,4},{6,7},{7,6},{8,9},{9,8},{10,11... | collective-permute-start | bytes 2359304 | tf_op jit(solution)/shard_map/ppermute | solution.py:23
  88.3 52.3 %collective-permute-start.2 = (bf16[128,3584]{1,0:T(8,128)(2,1)}, bf16[128,3584]{1,0:T(8,128)(2,1)}, u32[]{:S(2)}, u32[]{:S(2)}) collective-permute-start(bf16[128,3584]{1,0:T(8,128)(2,1)} %constant_dynamic-update-slice_fusion), channel_id=1, source_target_pairs={{0,16},{16,0},{32,48},{48,32},{64,80},{80,64},{96,112},{112,96},{1... | collective-permute-start | bytes 2752520 | tf_op jit(solution)/shard_map/ppermute | solution.py:19
  90.2 68.5 %collective-permute-start.3 = (bf16[128,3584]{1,0:T(8,128)(2,1)}, bf16[128,3584]{1,0:T(8,128)(2,1)}, u32[]{:S(2)}, u32[]{:S(2)}) collective-permute-start(bf16[128,3584]{1,0:T(8,128)(2,1)} %constant_dynamic-update-slice_fusion), channel_id=1, source_target_pairs={{0,12},{4,8},{8,4},{12,0},{1,13},{5,9},{9,5},{13,1},{2,14},{6,10},... | collective-permute-start | bytes 2752520 | tf_op jit(solution)/shard_map/ppermute | solution.py:19
  92.8 65.7 %collective-permute-start.11 = (s16[272,768]{1,0:T(8,128)(2,1)S(1)}, s16[272,768]{1,0:T(8,128)(2,1)S(1)}, u32[]{:S(2)}, u32[]{:S(2)}) collective-permute-start(s16[272,768]{1,0:T(8,128)(2,1)S(1)} %pad_add_fusion), channel_id=1, source_target_pairs={{0,2},{2,0},{1,3},{3,1},{4,6},{6,4},{5,7},{7,5},{8,10},{10,8},{9,1... | collective-permute-start | bytes 1253384 | tf_op jit(solution)/shard_map/ppermute | solution.py:23
  140.5 25.9 %collective-permute-start.4 = (bf16[128,3584]{1,0:T(8,128)(2,1)}, bf16[128,3584]{1,0:T(8,128)(2,1)}, u32[]{:S(2)}, u32[]{:S(2)}) collective-permute-start(bf16[128,3584]{1,0:T(8,128)(2,1)} %collective-permute-done.2), channel_id=1, source_target_pairs={{0,12},{4,8},{8,4},{12,0},{1,13},{5,9},{9,5},{13,1},{2,14},{6,10},... | collective-permute-start | bytes 2752520 | tf_op jit(solution)/shard_map/ppermute | solution.py:19
  158.7 4.8 %copy-start = (bf16[768,3584]{1,0:T(8,128)(2,1)S(1)}, bf16[768,3584]{1,0:T(8,128)(2,1)}, u32[]{:S(2)}) copy-start(bf16[768,3584]{1,0:T(8,128)(2,1)} %all-gather.2.cloned.1.call-done) | copy-start | bytes 16515076
  166.4 3.3 %copy-start.2 = (f32[256,768]{1,0:T(8,128)}, f32[256,768]{1,0:T(8,128)S(1)}, u32[]{:S(2)}) copy-start(f32[256,768]{1,0:T(8,128)S(1)} %fusion) | copy-start | bytes 2359300
  173.3 4.6 %copy-start.3 = (f32[256,768]{1,0:T(8,128)S(1)}, f32[256,768]{1,0:T(8,128)}, u32[]{:S(2)}) copy-start(f32[256,768]{1,0:T(8,128)} %copy-done.2) | copy-start | bytes 2359300
  173.3 4.3 %collective-permute-start.12 = (f32[256,768]{1,0:T(8,128)S(1)}, f32[256,768]{1,0:T(8,128)S(1)}, u32[]{:S(2)}, u32[]{:S(2)}) collective-permute-start(f32[256,768]{1,0:T(8,128)S(1)} %fusion.9), channel_id=1, source_target_pairs={{0,1},{1,0},{2,3},{3,2},{4,5},{5,4},{6,7},{7,6},{8,9},{9,8},{10,11... | collective-permute-start | bytes 2359304 | tf_op jit(solution)/shard_map/ppermute | solution.py:23
  178.3 3.1 %collective-permute-start.13 = (f32[2,2,16,96]{3,0,1,2:T(2,128)S(1)}, f32[2,2,16,96]{3,0,1,2:T(2,128)S(1)}, u32[]{:S(2)}, u32[]{:S(2)}) collective-permute-start(f32[2,2,16,96]{3,0,1,2:T(2,128)S(1)} %bitcast.51), channel_id=1, source_target_pairs={{0,1},{1,0},{2,3},{3,2},{4,5},{5,4},{6,7},{7,6},{8,9},{9,8},{10,11... | collective-permute-start | bytes 73736 | tf_op jit(solution)/shard_map/ppermute | solution.py:23
  181.4 5.6 %collective-permute-start.14 = (f32[2,16,96]{2,0,1:T(2,128)S(1)}, f32[2,16,96]{2,0,1:T(2,128)S(1)}, u32[]{:S(2)}, u32[]{:S(2)}) collective-permute-start(f32[2,16,96]{2,0,1:T(2,128)S(1)} %fusion.17), channel_id=1, source_target_pairs={{0,4},{4,0},{8,12},{12,8},{1,5},{5,1},{9,13},{13,9},{2,6},{6,2},{1... | collective-permute-start | bytes 36872 | tf_op jit(solution)/shard_map/ppermute | solution.py:19
  187.1 14.3 %collective-permute-start.15 = (f32[2,16,96]{2,1,0:T(8,128)S(1)}, f32[2,16,96]{2,1,0:T(8,128)S(1)}, u32[]{:S(2)}, u32[]{:S(2)}) collective-permute-start(f32[2,16,96]{2,1,0:T(8,128)S(1)} %bitcast.53), channel_id=1, source_target_pairs={{0,2},{2,0},{1,3},{3,1},{4,6},{6,4},{5,7},{7,5},{8,10},{10,8},{9,1... | collective-permute-start | bytes 36872 | tf_op jit(solution)/shard_map/ppermute | solution.py:23
Sparse Core Ops, SparseCore 0:
  9.4 89.1 all-gather.1

commit v5 on v3

--- a/solution.py
+++ b/solution.py
@@ -65,23 +65,21 @@
         second, jnp.concatenate([pair_inputs, token_inputs], axis=0), jnp.concatenate([token_inputs, pair_inputs], axis=0)
     )
     grads = lax.all_gather(token_grads, "y_lo", axis=0, tiled=True)
-    in_got = flip(in_factors, "z_lo", 4)
-    in_near = grow(grow(jnp.concatenate([in_factors, in_got], axis=0), 2), 1)
+    in_near = grow(grow(grow(in_factors, 4), 2), 1)
     in_far = flip(in_near, Y, FACTORS_BY)
     blocks, sent = coded_half(split_sum(rows_of(inputs, in_near), rows_of(inputs, in_far), core))
     right = sum_over_halves(blocks, sent)
 
-    up_near = grow(grow(after(up_factors, in_got), 4), 2)
+    up_near = grow(grow(up_factors, 4), 2)
     next_near = flip(up_near, "z_lo", 1)
     up_far = flip(up_near, Y, FACTORS_BY)
     next_far = flip(next_near, Y, FACTORS_BY)
-    left = lax.optimization_barrier(rows_of(grads, jnp.concatenate([up_near, next_near, up_far, next_far], axis=0)))
     right = right.reshape(-1, 2 * tokens)
+    other = swap(after(right, up_far[:1, :1] + next_far[:1, :1]), "core")
+    right_near, right_far = jnp.where(core == 0, right, other), jnp.where(core == 0, other, right)
+    ups = jnp.concatenate([up_near, next_near, up_far, next_far], axis=0)
+    left = lax.optimization_barrier(rows_of(grads, ups))
     half = right.shape[0]
-    head, rest = right[: half // 2], right[half // 2 :]
-    other = swap(head, "core")
-    other = jnp.concatenate([other, swap(after(rest, left[:1, :1] + other[:1, :1]), "core")], axis=0)
-    right_near, right_far = jnp.where(core == 0, right, other), jnp.where(core == 0, other, right)
     summed = jnp.concatenate([scores_of(left[:half], right_near), scores_of(left[half:], right_far)], axis=0)
 
     count = summed.shape[0]

time: 209 us -> 198 us (0.947)
  the two profiles are of different devices: /device:TPU:32 before, /device:TPU:36 now
where the time goes in v5:
time: 198 us; the launch traced here: 197 us
  waiting for transfers between devices  87.9 us (44%)
  starting transfers between devices  69.9 us (35%)
  between operations  15.1 us (8%)
  matrix products  13.1 us (7%)
  local copies, waits for them, and re-layouts  8.01 us (4%)
  other arithmetic  3.16 us (2%)
    ppermute x11, starting transfers between devices, flip(): lax.ppermute(value, axes, [(i, i ^ bits) for i in range(lax.axis_size(axe...  57.4 us
    ppermute x5, waiting for transfers between devices, swap(): return lax.ppermute(value, axis, SWAP)  52.5 us
    ppermute x11, waiting for transfers between devices, flip(): lax.ppermute(value, axes, [(i, i ^ bits) for i in range(lax.axis_size(axe...  35.4 us
    ppermute x5, starting transfers between devices, swap(): return lax.ppermute(value, axis, SWAP)  12.6 us
    dot_general x3, matrix products, rows_of(): lax.dot_general(factor_rows, data_rows, (((1,), (1,)), ((), ())), preferr...  12.2 us
    unnamed x14, local copies, waits for them, and re-layouts  5.63 us
  transfers between devices with their start and end apart: 17, of which 9 were waited for; matrix products, arithmetic and copies ran while one was open for 11% of the time, Pallas kernels for 0%

profile of v5, /device:TPU:36, one launch (start us, length us, event | category | flops | bytes accessed | tf_op | source)
XLA Modules:
  0.0 197.2 jit_solution(1807877084598129380)
XLA Ops:
  6.5 9.2 %collective-permute-start.5 = (bf16[32,1024]{1,0:T(8,128)(2,1)}, bf16[32,1024]{1,0:T(8,128)(2,1)S(1)}, u32[]{:S(2)}, u32[]{:S(2)}) collective-permute-start(bf16[32,1024]{1,0:T(8,128)(2,1)} %param.8), channel_id=1, source_target_pairs={{0,64},{16,80},{32,96},{48,112},{64,0},{80,16},{96,32},{112,48},{1... | collective-permute-start | bytes 196616 | tf_op jit(solution)/shard_map/ppermute | solution.py:19
  15.8 3.5 %collective-permute-start.8 = (bf16[384,1024]{1,0:T(8,128)(2,1)}, bf16[384,1024]{1,0:T(8,128)(2,1)}, u32[]{:S(2)}, u32[]{:S(2)}) collective-permute-start(bf16[384,1024]{1,0:T(8,128)(2,1)} %param.6), channel_id=1, source_target_pairs={{0,4},{4,0},{8,12},{12,8},{1,5},{5,1},{9,13},{13,9},{2,6},{6,2},{1... | collective-permute-start | bytes 2359304 | tf_op jit(solution)/shard_map/ppermute | solution.py:19
  23.0 17.3 %collective-permute-start.6 = (bf16[64,1024]{1,0:T(8,128)(2,1)S(1)}, bf16[64,1024]{1,0:T(8,128)(2,1)S(1)}, u32[]{:S(2)}, u32[]{:S(2)}) collective-permute-start(bf16[64,1024]{1,0:T(8,128)(2,1)S(1)} %pad_maximum_fusion.2), channel_id=1, source_target_pairs={{0,32},{16,48},{32,0},{48,16},{64,96},{80,112},{96,64},{112,80},{1... | collective-permute-start | bytes 393224 | tf_op jit(solution)/shard_map/ppermute | solution.py:19
  40.3 7.9 %collective-permute-done.6 = bf16[64,1024]{1,0:T(8,128)(2,1)S(1)} collective-permute-done((bf16[64,1024]{1,0:T(8,128)(2,1)S(1)}, bf16[64,1024]{1,0:T(8,128)(2,1)S(1)}, u32[]{:S(2)}, u32[]{:S(2)}) %collective-permute-start.6) | collective-permute-done | bytes 131104 | tf_op jit(solution)/shard_map/ppermute | solution.py:19
  48.3 1.9 collective-permute-start.7
  50.3 1.9 collective-permute-start.1
  53.0 6.3 %collective-permute-done.7 = bf16[128,1024]{1,0:T(8,128)(2,1)S(1)} collective-permute-done((bf16[128,1024]{1,0:T(8,128)(2,1)S(1)}, bf16[128,1024]{1,0:T(8,128)(2,1)S(1)}, u32[]{:S(2)}, u32[]{:S(2)}) %collective-permute-start.7) | collective-permute-done | bytes 262176 | tf_op jit(solution)/shard_map/ppermute | solution.py:19
  59.4 4.1 %collective-permute-start.9 = (bf16[256,1024]{1,0:T(8,128)(2,1)S(1)}, bf16[256,1024]{1,0:T(8,128)(2,1)S(1)}, u32[]{:S(2)}, u32[]{:S(2)}) collective-permute-start(bf16[256,1024]{1,0:T(8,128)(2,1)S(1)} %constant_dynamic-update-slice_fusion.9), channel_id=1, source_target_pairs={{0,12},{4,8},{8,4},{12,0},{1,13},{5,9},{9,5},{13,1},{2,14},{6,10},... | collective-permute-start | bytes 1572872 | tf_op jit(solution)/shard_map/ppermute | solution.py:19
  63.5 8.9 %collective-permute-done.1 = bf16[64,3584]{1,0:T(8,128)(2,1)S(1)} collective-permute-done((bf16[64,3584]{1,0:T(8,128)(2,1)S(1)}, bf16[64,3584]{1,0:T(8,128)(2,1)S(1)}, u32[]{:S(2)}, u32[]{:S(2)}) %collective-permute-start.1) | collective-permute-done | bytes 458784 | tf_op jit(solution)/shard_map/ppermute | solution.py:19
  73.3 6.7 %collective-permute-start.2 = (bf16[128,3584]{1,0:T(8,128)(2,1)}, bf16[128,3584]{1,0:T(8,128)(2,1)S(1)}, u32[]{:S(2)}, u32[]{:S(2)}) collective-permute-start(bf16[128,3584]{1,0:T(8,128)(2,1)} %get-tuple-element.12), channel_id=1, source_target_pairs={{0,16},{16,0},{32,48},{48,32},{64,80},{80,64},{96,112},{112,96},{1... | collective-permute-start | bytes 2752520 | tf_op jit(solution)/shard_map/ppermute | solution.py:19
  80.0 4.1 %collective-permute-start.3 = (bf16[128,3584]{1,0:T(8,128)(2,1)}, bf16[128,3584]{1,0:T(8,128)(2,1)S(1)}, u32[]{:S(2)}, u32[]{:S(2)}) collective-permute-start(bf16[128,3584]{1,0:T(8,128)(2,1)} %get-tuple-element.12), channel_id=1, source_target_pairs={{0,12},{4,8},{8,4},{12,0},{1,13},{5,9},{9,5},{13,1},{2,14},{6,10},... | collective-permute-start | bytes 2752520 | tf_op jit(solution)/shard_map/ppermute | solution.py:19
  84.2 2.6 %fusion.4 = f32[256,768]{1,0:T(8,128)S(1)} fusion(bf16[256,1024]{1,0:T(8,128)(2,1)S(1)} %constant_dynamic-update-slice_fusion.9, bf16[384,1024]{1,0:T(8,128)(2,1)} %param.6, bf16[384,1024]{1,0:T(8,128)(2,1)} %collective-permute-done.8, pred[]{:T(512)S(6)} %eq.236), kind=kOutput, calls=%fused_computation.18 | convolution fusion | flops 409731072 | bytes 2883585 | tf_op jit(solution)/shard_map/dot_general | solution.py:15
  86.8 2.9 %broadcast_select_fusion.1 = (f32[256,768]{1,0:T(8,128)}, f32[256,768]{1,0:T(8,128)S(1)}) fusion(f32[256,768]{1,0:T(8,128)S(1)} %fusion.4, pred[]{:T(512)S(6)} %eq.237, bf16[256,1024]{1,0:T(8,128)(2,1)S(1)} %collective-permute-done.9, bf16[384,1024]{1,0:T(8,128)(2,1)S(1)} %copy-done.2, bf16[384,1024]{1,0:T(8,128)(2,1)} %collective-permute-done.8, pred[]{:T(512)S(6)} %eq.236), kind=kOutput, calls=%fused_computation.16 | convolution fusion | flops 409927680 | bytes 4456450 | tf_op jit(solution)/shard_map/dot_general | solution.py:15
  91.6 8.8 %collective-permute-done.2 = bf16[128,3584]{1,0:T(8,128)(2,1)S(1)} collective-permute-done((bf16[128,3584]{1,0:T(8,128)(2,1)}, bf16[128,3584]{1,0:T(8,128)(2,1)S(1)}, u32[]{:S(2)}, u32[]{:S(2)}) %collective-permute-start.2) | collective-permute-done | bytes 917536 | tf_op jit(solution)/shard_map/ppermute | solution.py:19
  100.4 4.1 %collective-permute-start.4 = (bf16[128,3584]{1,0:T(8,128)(2,1)S(1)}, bf16[128,3584]{1,0:T(8,128)(2,1)S(1)}, u32[]{:S(2)}, u32[]{:S(2)}) collective-permute-start(bf16[128,3584]{1,0:T(8,128)(2,1)S(1)} %collective-permute-done.2), channel_id=1, source_target_pairs={{0,12},{4,8},{8,4},{12,0},{1,13},{5,9},{9,5},{13,1},{2,14},{6,10},... | collective-permute-start | bytes 2752520 | tf_op jit(solution)/shard_map/ppermute | solution.py:19
  108.0 4.1 %collective-permute-start.11 = (s16[272,768]{1,0:T(8,128)(2,1)S(1)}, s16[272,768]{1,0:T(8,128)(2,1)S(1)}, u32[]{:S(2)}, u32[]{:S(2)}) collective-permute-start(s16[272,768]{1,0:T(8,128)(2,1)S(1)} %pad_add_fusion), channel_id=1, source_target_pairs={{0,2},{2,0},{1,3},{3,1},{4,6},{6,4},{5,7},{7,5},{8,10},{10,8},{9,1... | collective-permute-start | bytes 1253384 | tf_op jit(solution)/shard_map/ppermute | solution.py:23
  113.2 40.4 %collective-permute-done.11 = s16[272,768]{1,0:T(8,128)(2,1)S(1)} collective-permute-done((s16[272,768]{1,0:T(8,128)(2,1)S(1)}, s16[272,768]{1,0:T(8,128)(2,1)S(1)}, u32[]{:S(2)}, u32[]{:S(2)}) %collective-permute-start.11) | collective-permute-done | bytes 417824 | tf_op jit(solution)/shard_map/ppermute | solution.py:23
  155.8 1.9 collective-permute-start.12
  158.8 6.7 %fusion.46 = f32[512,768]{1,0:T(8,128)S(1)} fusion(bf16[512,3584]{1,0:T(8,128)(2,1)} %constant_dynamic-update-slice_fusion.3, bf16[768,3584]{1,0:T(8,128)(2,1)} %all-gather.2.cloned.1.call-done), kind=kOutput, calls=%fused_computation.120 | convolution fusion | flops 2818572288 | bytes 10747904 | tf_op jit(solution)/shard_map/dot_general | solution.py:15
  166.2 2.4 %collective-permute-start.13 = (f32[2,2,16,96]{3,0,1,2:T(2,128)S(1)}, f32[2,2,16,96]{3,0,1,2:T(2,128)S(1)}, u32[]{:S(2)}, u32[]{:S(2)}) collective-permute-start(f32[2,2,16,96]{3,0,1,2:T(2,128)S(1)} %bitcast.47), channel_id=1, source_target_pairs={{0,1},{1,0},{2,3},{3,2},{4,5},{5,4},{6,7},{7,6},{8,9},{9,8},{10,11... | collective-permute-start | bytes 73736 | tf_op jit(solution)/shard_map/ppermute | solution.py:23
  169.5 2.7 %collective-permute-start.14 = (f32[2,16,96]{2,0,1:T(2,128)S(1)}, f32[2,16,96]{2,0,1:T(2,128)S(1)}, u32[]{:S(2)}, u32[]{:S(2)}) collective-permute-start(f32[2,16,96]{2,0,1:T(2,128)S(1)} %fusion.8), channel_id=1, source_target_pairs={{0,4},{4,0},{8,12},{12,8},{1,5},{5,1},{9,13},{13,9},{2,6},{6,2},{1... | collective-permute-start | bytes 36872 | tf_op jit(solution)/shard_map/ppermute | solution.py:19
  172.1 2.9 %collective-permute-done.14 = f32[2,16,96]{2,0,1:T(2,128)S(1)} collective-permute-done((f32[2,16,96]{2,0,1:T(2,128)S(1)}, f32[2,16,96]{2,0,1:T(2,128)S(1)}, u32[]{:S(2)}, u32[]{:S(2)}) %collective-permute-start.14) | collective-permute-done | bytes 12320 | tf_op jit(solution)/shard_map/ppermute | solution.py:19
  175.1 2.2 %collective-permute-start.15 = (f32[2,16,96]{2,1,0:T(8,128)S(1)}, f32[2,16,96]{2,1,0:T(8,128)S(1)}, u32[]{:S(2)}, u32[]{:S(2)}) collective-permute-start(f32[2,16,96]{2,1,0:T(8,128)S(1)} %bitcast.49), channel_id=1, source_target_pairs={{0,2},{2,0},{1,3},{3,1},{4,6},{6,4},{5,7},{7,5},{8,10},{10,8},{9,1... | collective-permute-start | bytes 36872 | tf_op jit(solution)/shard_map/ppermute | solution.py:23
  177.4 12.1 %collective-permute-done.15 = f32[2,16,96]{2,1,0:T(8,128)S(1)} collective-permute-done((f32[2,16,96]{2,1,0:T(8,128)S(1)}, f32[2,16,96]{2,1,0:T(8,128)S(1)}, u32[]{:S(2)}, u32[]{:S(2)}) %collective-permute-start.15) | collective-permute-done | bytes 12320 | tf_op jit(solution)/shard_map/ppermute | solution.py:23
  (54 shorter events, 16.5 us)
Async XLA Ops:
  6.5 16.4 %copy-start.1 = (bf16[32,1024]{1,0:T(8,128)(2,1)S(1)}, bf16[32,1024]{1,0:T(8,128)(2,1)}, u32[]{:S(2)}) copy-start(bf16[32,1024]{1,0:T(8,128)(2,1)} %param.8) | copy-start | bytes 196612
  6.5 43.7 %copy-start = (bf16[32,3584]{1,0:T(8,128)(2,1)S(1)}, bf16[32,3584]{1,0:T(8,128)(2,1)}, u32[]{:S(2)}) copy-start(bf16[32,3584]{1,0:T(8,128)(2,1)} %param.7) | copy-start | bytes 688132
  6.5 152.3 %all-gather.2.cloned.1.call-start = ((), (), s32[]{:S(2)}) async-start(), calls=%async_computation | async-start | bytes 8257536 | tf_op jit(solution)/shard_map/all_gather | solution.py:67
  6.5 16.4 %collective-permute-start.5 = (bf16[32,1024]{1,0:T(8,128)(2,1)}, bf16[32,1024]{1,0:T(8,128)(2,1)S(1)}, u32[]{:S(2)}, u32[]{:S(2)}) collective-permute-start(bf16[32,1024]{1,0:T(8,128)(2,1)} %param.8), channel_id=1, source_target_pairs={{0,64},{16,80},{32,96},{48,112},{64,0},{80,16},{96,32},{112,48},{1... | collective-permute-start | bytes 196616 | tf_op jit(solution)/shard_map/ppermute | solution.py:19
  15.8 68.4 %collective-permute-start.8 = (bf16[384,1024]{1,0:T(8,128)(2,1)}, bf16[384,1024]{1,0:T(8,128)(2,1)}, u32[]{:S(2)}, u32[]{:S(2)}) collective-permute-start(bf16[384,1024]{1,0:T(8,128)(2,1)} %param.6), channel_id=1, source_target_pairs={{0,4},{4,0},{8,12},{12,8},{1,5},{5,1},{9,13},{13,9},{2,6},{6,2},{1... | collective-permute-start | bytes 2359304 | tf_op jit(solution)/shard_map/ppermute | solution.py:19
  19.3 31.0 %collective-permute-start = (bf16[32,3584]{1,0:T(8,128)(2,1)}, bf16[32,3584]{1,0:T(8,128)(2,1)S(1)}, u32[]{:S(2)}, u32[]{:S(2)}) collective-permute-start(bf16[32,3584]{1,0:T(8,128)(2,1)} %param.7), channel_id=1, source_target_pairs={{0,64},{16,80},{32,96},{48,112},{64,0},{80,16},{96,32},{112,48},{1... | collective-permute-start | bytes 688136 | tf_op jit(solution)/shard_map/ppermute | solution.py:19
  23.0 25.3 %collective-permute-start.6 = (bf16[64,1024]{1,0:T(8,128)(2,1)S(1)}, bf16[64,1024]{1,0:T(8,128)(2,1)S(1)}, u32[]{:S(2)}, u32[]{:S(2)}) collective-permute-start(bf16[64,1024]{1,0:T(8,128)(2,1)S(1)} %pad_maximum_fusion.2), channel_id=1, source_target_pairs={{0,32},{16,48},{32,0},{48,16},{64,96},{80,112},{96,64},{112,80},{1... | collective-permute-start | bytes 393224 | tf_op jit(solution)/shard_map/ppermute | solution.py:19
  48.3 11.1 %collective-permute-start.7 = (bf16[128,1024]{1,0:T(8,128)(2,1)S(1)}, bf16[128,1024]{1,0:T(8,128)(2,1)S(1)}, u32[]{:S(2)}, u32[]{:S(2)}) collective-permute-start(bf16[128,1024]{1,0:T(8,128)(2,1)S(1)} %pad_maximum_fusion.1), channel_id=1, source_target_pairs={{0,16},{16,0},{32,48},{48,32},{64,80},{80,64},{96,112},{112,96},{1... | collective-permute-start | bytes 786440 | tf_op jit(solution)/shard_map/ppermute | solution.py:19
  50.3 22.0 %collective-permute-start.1 = (bf16[64,3584]{1,0:T(8,128)(2,1)S(1)}, bf16[64,3584]{1,0:T(8,128)(2,1)S(1)}, u32[]{:S(2)}, u32[]{:S(2)}) collective-permute-start(bf16[64,3584]{1,0:T(8,128)(2,1)S(1)} %pad_maximum_fusion), channel_id=1, source_target_pairs={{0,32},{16,48},{32,0},{48,16},{64,96},{80,112},{96,64},{112,80},{1... | collective-permute-start | bytes 1376264 | tf_op jit(solution)/shard_map/ppermute | solution.py:19
  59.4 27.4 %collective-permute-start.9 = (bf16[256,1024]{1,0:T(8,128)(2,1)S(1)}, bf16[256,1024]{1,0:T(8,128)(2,1)S(1)}, u32[]{:S(2)}, u32[]{:S(2)}) collective-permute-start(bf16[256,1024]{1,0:T(8,128)(2,1)S(1)} %constant_dynamic-update-slice_fusion.9), channel_id=1, source_target_pairs={{0,12},{4,8},{8,4},{12,0},{1,13},{5,9},{9,5},{13,1},{2,14},{6,10},... | collective-permute-start | bytes 1572872 | tf_op jit(solution)/shard_map/ppermute | solution.py:19
  73.3 13.4 %copy-start.2 = (bf16[384,1024]{1,0:T(8,128)(2,1)S(1)}, bf16[384,1024]{1,0:T(8,128)(2,1)}, u32[]{:S(2)}) copy-start(bf16[384,1024]{1,0:T(8,128)(2,1)} %param.6) | copy-start | bytes 2359300
  73.3 27.1 %collective-permute-start.2 = (bf16[128,3584]{1,0:T(8,128)(2,1)}, bf16[128,3584]{1,0:T(8,128)(2,1)S(1)}, u32[]{:S(2)}, u32[]{:S(2)}) collective-permute-start(bf16[128,3584]{1,0:T(8,128)(2,1)} %get-tuple-element.12), channel_id=1, source_target_pairs={{0,16},{16,0},{32,48},{48,32},{64,80},{80,64},{96,112},{112,96},{1... | collective-permute-start | bytes 2752520 | tf_op jit(solution)/shard_map/ppermute | solution.py:19
  80.0 24.9 %collective-permute-start.3 = (bf16[128,3584]{1,0:T(8,128)(2,1)}, bf16[128,3584]{1,0:T(8,128)(2,1)S(1)}, u32[]{:S(2)}, u32[]{:S(2)}) collective-permute-start(bf16[128,3584]{1,0:T(8,128)(2,1)} %get-tuple-element.12), channel_id=1, source_target_pairs={{0,12},{4,8},{8,4},{12,0},{1,13},{5,9},{9,5},{13,1},{2,14},{6,10},... | collective-permute-start | bytes 2752520 | tf_op jit(solution)/shard_map/ppermute | solution.py:19
  89.7 16.8 %collective-permute-start.10 = (f32[256,768]{1,0:T(8,128)}, f32[256,768]{1,0:T(8,128)}, u32[]{:S(2)}, u32[]{:S(2)}) collective-permute-start(f32[256,768]{1,0:T(8,128)} %get-tuple-element.23), channel_id=1, source_target_pairs={{0,1},{1,0},{2,3},{3,2},{4,5},{5,4},{6,7},{7,6},{8,9},{9,8},{10,11... | collective-permute-start | bytes 2359304 | tf_op jit(solution)/shard_map/ppermute | solution.py:23
  100.4 53.3 %collective-permute-start.4 = (bf16[128,3584]{1,0:T(8,128)(2,1)S(1)}, bf16[128,3584]{1,0:T(8,128)(2,1)S(1)}, u32[]{:S(2)}, u32[]{:S(2)}) collective-permute-start(bf16[128,3584]{1,0:T(8,128)(2,1)S(1)} %collective-permute-done.2), channel_id=1, source_target_pairs={{0,12},{4,8},{8,4},{12,0},{1,13},{5,9},{9,5},{13,1},{2,14},{6,10},... | collective-permute-start | bytes 2752520 | tf_op jit(solution)/shard_map/ppermute | solution.py:19
  108.0 45.6 %collective-permute-start.11 = (s16[272,768]{1,0:T(8,128)(2,1)S(1)}, s16[272,768]{1,0:T(8,128)(2,1)S(1)}, u32[]{:S(2)}, u32[]{:S(2)}) collective-permute-start(s16[272,768]{1,0:T(8,128)(2,1)S(1)} %pad_add_fusion), channel_id=1, source_target_pairs={{0,2},{2,0},{1,3},{3,1},{4,6},{6,4},{5,7},{7,5},{8,10},{10,8},{9,1... | collective-permute-start | bytes 1253384 | tf_op jit(solution)/shard_map/ppermute | solution.py:23
  155.8 9.7 %collective-permute-start.12 = (f32[256,768]{1,0:T(8,128)S(1)}, f32[256,768]{1,0:T(8,128)S(1)}, u32[]{:S(2)}, u32[]{:S(2)}) collective-permute-start(f32[256,768]{1,0:T(8,128)S(1)} %get-tuple-element.7), channel_id=1, source_target_pairs={{0,1},{1,0},{2,3},{3,2},{4,5},{5,4},{6,7},{7,6},{8,9},{9,8},{10,11... | collective-permute-start | bytes 2359304 | tf_op jit(solution)/shard_map/ppermute | solution.py:23
  166.2 3.3 %collective-permute-start.13 = (f32[2,2,16,96]{3,0,1,2:T(2,128)S(1)}, f32[2,2,16,96]{3,0,1,2:T(2,128)S(1)}, u32[]{:S(2)}, u32[]{:S(2)}) collective-permute-start(f32[2,2,16,96]{3,0,1,2:T(2,128)S(1)} %bitcast.47), channel_id=1, source_target_pairs={{0,1},{1,0},{2,3},{3,2},{4,5},{5,4},{6,7},{7,6},{8,9},{9,8},{10,11... | collective-permute-start | bytes 73736 | tf_op jit(solution)/shard_map/ppermute | solution.py:23
  169.5 5.6 %collective-permute-start.14 = (f32[2,16,96]{2,0,1:T(2,128)S(1)}, f32[2,16,96]{2,0,1:T(2,128)S(1)}, u32[]{:S(2)}, u32[]{:S(2)}) collective-permute-start(f32[2,16,96]{2,0,1:T(2,128)S(1)} %fusion.8), channel_id=1, source_target_pairs={{0,4},{4,0},{8,12},{12,8},{1,5},{5,1},{9,13},{13,9},{2,6},{6,2},{1... | collective-permute-start | bytes 36872 | tf_op jit(solution)/shard_map/ppermute | solution.py:19
  175.1 14.3 %collective-permute-start.15 = (f32[2,16,96]{2,1,0:T(8,128)S(1)}, f32[2,16,96]{2,1,0:T(8,128)S(1)}, u32[]{:S(2)}, u32[]{:S(2)}) collective-permute-start(f32[2,16,96]{2,1,0:T(8,128)S(1)} %bitcast.49), channel_id=1, source_target_pairs={{0,2},{2,0},{1,3},{3,1},{4,6},{6,4},{5,7},{7,5},{8,10},{10,8},{9,1... | collective-permute-start | bytes 36872 | tf_op jit(solution)/shard_map/ppermute | solution.py:23
Sparse Core Ops, SparseCore 0:
  21.3 84.2 all-gather.1
